TPU v7x, 32 devices: a whole 2x2x4 slice. The times are simulated.
32 devices in a mesh: dp: 8 (over z, y), tensor: 4 (over x, core).
Axes of the slice: x: 2, y: 2, z: 4, core: 2. Of those that a mesh axis runs over, the one named last changes fastest.
Arguments:
- frames: bfloat16 [64, 13, 13, 512], P('dp', None, None, 'tensor'), may hold values from -10 to 10
- item_mask: int32 [64], P('dp'), may hold values 0 or 1
- weights: float32 [2, 4608, 512], P(None, 'dp', 'tensor'), may hold values from -0.09375 to 0.09375
- biases: float32 [2, 512], replicated, may hold values from -0.4 to 0.4
- cotangent: bfloat16 [64, 13, 13, 512], P('dp', None, None, 'tensor'), may hold values from -8 to 8
- weight_first: float32 [2, 4608, 512], P(None, 'dp', 'tensor'), may hold values from -0.0018412241 to 0.0018412241
- weight_second: float32 [2, 4608, 512], P(None, 'dp', 'tensor'), may hold values from 1.0594082e-07 to 1.6950531e-06
- bias_first: float32 [2, 512], replicated, may hold values from -0.0018412241 to 0.0018412241
- bias_second: float32 [2, 512], replicated, may hold values from 1.0594082e-07 to 1.6950531e-06
Outputs:
- act4: bfloat16 [64, 13, 13, 512], P('dp', None, None, 'tensor')
- act5: bfloat16 [64, 13, 13, 512], P('dp', None, None, 'tensor')
- input_grad: float32 [64, 13, 13, 512], P('dp', None, None, 'tensor')
- grad_norm: float32 [], replicated
- new_weights: float32 [2, 4608, 512], P(None, 'dp', 'tensor')
- new_weight_first: float32 [2, 4608, 512], P(None, 'dp', 'tensor')
- new_weight_second: float32 [2, 4608, 512], P(None, 'dp', 'tensor')
- new_biases: float32 [2, 512], replicated
- new_bias_first: float32 [2, 512], replicated
- new_bias_second: float32 [2, 512], replicated
All inputs are finite; a program needn't handle non-finite values. No bound on the sum of `item_mask` on one device may be relied on, other than what follows from the above.
Results may differ from a plain program's by a relative error of at most 0.0086.
Values may be sent and summed in bfloat16 or wider, within the bound.
A program may use at most 128 MiB of HBM per device.

v0:
```python
import jax
import jax.numpy as jnp
from jax import lax
from jax.sharding import PartitionSpec as P

STEP = 5


CLIP_NORM = 1.0
BETA_ONE = 0.5
BETA_TWO = 0.5
RATE = 0.01
BIAS_RATE = 0.03
DECAY = 0.1
EPSILON = 1e-08


def split_up(shard, dim, devices):
    before, after = (shard.shape[:dim], shard.shape[dim + 1 :])
    return jnp.moveaxis(shard.reshape(*before, devices, -1, *after), dim, 0)


def sent_and_summed(shard, axis, dim):
    parts = split_up(shard, dim, lax.axis_size(axis))
    arrived = lax.all_to_all(parts, axis, split_axis=0, concat_axis=0, tiled=True)
    return arrived.astype(jnp.float32).sum(axis=0)


def to_kernel(weight_rows):
    in_chan = weight_rows.shape[0] // 9
    return jnp.transpose(weight_rows.reshape(in_chan, 3, 3, weight_rows.shape[1]), (1, 2, 0, 3))


def flipped(kernel):
    return jnp.transpose(kernel[::-1, ::-1], (0, 1, 3, 2))


def convolve(inputs, kernel):
    return lax.conv_general_dilated(
        inputs,
        kernel,
        (1, 1),
        ((1, 1), (1, 1)),
        dimension_numbers=("NHWC", "HWIO", "NHWC"),
        preferred_element_type=jnp.float32,
    )


def kernel_grad(inputs, deltas):
    height, map_width = (inputs.shape[1], inputs.shape[2])
    padded = jnp.pad(inputs, ((0, 0), (1, 1), (1, 1), (0, 0)))
    flat_deltas = deltas.reshape(-1, deltas.shape[3])
    pieces = []
    for offset in range(9):
        row_off, col_off = (offset // 3, offset % 3)
        shifted = padded[:, row_off : row_off + height, col_off : col_off + map_width, :].reshape(
            -1, inputs.shape[3]
        )
        pieces.append(
            lax.dot_general(
                shifted, flat_deltas, (((0,), (0,)), ((), ())), preferred_element_type=jnp.float32
            )
        )
    return jnp.stack(pieces, axis=1).reshape(-1, deltas.shape[3])


def gelu_back(pre_act, upstream):
    unused, pullback = jax.vjp(jax.nn.gelu, pre_act)
    return pullback(upstream)[0]


def bias_sums(delta_four, delta_five):
    return jnp.stack(
        [
            jnp.sum(delta_four, axis=(0, 1, 2), dtype=jnp.float32),
            jnp.sum(delta_five, axis=(0, 1, 2), dtype=jnp.float32),
        ]
    )


def gather_channels(acts):
    return lax.all_gather(acts, "tensor", axis=3, tiled=True)


def sum_channels(partial_sum):
    return lax.psum_scatter(partial_sum, "tensor", scatter_dimension=3, tiled=True)


def adam_update(param, grad, first, second, rate, decay):
    first_new = BETA_ONE * first + (1.0 - BETA_ONE) * grad
    second_new = BETA_TWO * second + (1.0 - BETA_TWO) * grad * grad
    corrected = first_new / (1.0 - BETA_ONE**STEP)
    scaled = jnp.sqrt(second_new / (1.0 - BETA_TWO**STEP)) + EPSILON
    return (param - rate * (corrected / scaled + decay * param), first_new, second_new)


def on_device(
    frames,
    item_mask,
    weights,
    biases,
    cotangent,
    weight_first,
    weight_second,
    bias_first,
    bias_second,
):
    rows_low = lax.all_gather(weights.astype(jnp.bfloat16), "dp", axis=1, tiled=True)
    mask_float = item_mask.astype(jnp.float32)[:, None, None, None]
    local_chan = frames.shape[3]
    tensor_rank = lax.axis_index("tensor")
    kernel_four = to_kernel(rows_low[0])
    kernel_five = to_kernel(rows_low[1])
    back_kernels = (flipped(kernel_four), flipped(kernel_five))

    def back_project(deltas, layer):
        return sum_channels(convolve(deltas, back_kernels[layer]))

    own_bias = lax.dynamic_slice_in_dim(biases, tensor_rank * local_chan, local_chan, 1)
    full_in = gather_channels(frames)
    pre_four = convolve(full_in, kernel_four) + own_bias[0]
    act_four = jax.nn.gelu(pre_four).astype(jnp.bfloat16)
    full_mid = gather_channels(act_four)
    pre_five = convolve(full_mid, kernel_five) + own_bias[1]
    act_five = (mask_float * jax.nn.gelu(pre_five)).astype(jnp.bfloat16)
    delta_five = gelu_back(pre_five, cotangent.astype(jnp.float32) * mask_float).astype(
        jnp.bfloat16
    )
    grad_five = kernel_grad(full_mid, delta_five)
    back_four = back_project(delta_five, 1)
    delta_four = gelu_back(pre_four, back_four).astype(jnp.bfloat16)
    grad_four = kernel_grad(full_in, delta_four)
    input_grad = back_project(delta_four, 0)
    local_grads = jnp.stack([grad_four, grad_five])
    placed = lax.dynamic_update_slice_in_dim(
        jnp.zeros(biases.shape, jnp.float32),
        bias_sums(delta_four, delta_five),
        tensor_rank * local_chan,
        1,
    )
    grad_shard = sent_and_summed(local_grads.astype(jnp.bfloat16), "dp", 1)
    bias_grad, weight_squares = lax.psum(
        (placed, jnp.sum(grad_shard * grad_shard)), ("dp", "tensor")
    )
    grad_norm = jnp.sqrt(weight_squares + jnp.sum(bias_grad * bias_grad))
    factor = jnp.minimum(1.0, CLIP_NORM / (grad_norm + 1e-06))
    new_weights, weight_m, weight_v = adam_update(
        weights, grad_shard * factor, weight_first, weight_second, RATE, DECAY
    )
    new_biases, bias_m, bias_v = adam_update(
        biases, bias_grad * factor, bias_first, bias_second, BIAS_RATE, 0.0
    )
    return (
        act_four,
        act_five,
        input_grad,
        grad_norm,
        new_weights,
        weight_m,
        weight_v,
        new_biases,
        bias_m,
        bias_v,
    )


def solution(mesh):
    in_specs = (
        P("dp", None, None, "tensor"),
        P("dp"),
        P(None, "dp", "tensor"),
        P(),
        P("dp", None, None, "tensor"),
        P(None, "dp", "tensor"),
        P(None, "dp", "tensor"),
        P(),
        P(),
    )
    out_specs = (
        P("dp", None, None, "tensor"),
        P("dp", None, None, "tensor"),
        P("dp", None, None, "tensor"),
        P(),
        P(None, "dp", "tensor"),
        P(None, "dp", "tensor"),
        P(None, "dp", "tensor"),
        P(),
        P(),
        P(),
    )
    return jax.shard_map(
        on_device, mesh=mesh, in_specs=in_specs, out_specs=out_specs, check_vma=False
    )
```

profile of v0, /device:TPU:0, one launch (start us, length us, event | category | flops | bytes accessed | tf_op | source)
XLA Modules:
  0.0 284.3 jit_solution(3918558616718532981)
XLA Ops:
  7.2 0.0 copy-start.3
  7.2 0.0 all-gather.6.cloned.1.call-start
  7.2 1.8 convert_element_type.35
  9.1 0.0 all-gather.6.cloned.1.call-update
  9.1 0.0 all-gather.4.cloned.1.call-start
  9.1 0.7 all-gather.4.cloned.1.call-update
  9.8 0.0 all-gather.8.cloned.1.call-start
  9.9 0.0 copy-done.3
  9.9 55.7 %all-gather.6.cloned.1.call-done = bf16[2,4608,128]{2,1,0:T(8,128)(2,1)} async-done(((bf16[2,576,128]{2,1,0:T(8,128)(2,1)}), bf16[2,4608,128]{2,1,0:T(8,128)(2,1)}) %all-gather.6.cloned.1.call-update) | async-done | bytes 2359312 | tf_op jit(solution)/shard_map/all_gather | solution.py:108
  65.6 1.8 fusion.80
  67.4 1.9 reshape_squeeze.6
  69.3 15.1 %all-gather.4.cloned.1.call-done = bf16[8,13,13,512]{3,0,2,1:T(8,128)(2,1)} async-done(((bf16[8,13,13,128]{3,0,2,1:T(8,128)(2,1)}), bf16[8,13,13,512]{3,0,2,1:T(8,128)(2,1)}) %all-gather.4.cloned.1.call-update) | async-done | bytes 1384464 | tf_op jit(solution)/shard_map/all_gather | solution.py:82
  84.5 6.2 %multiply_convert_fusion.1 = (bf16[8,13,13,128]{3,0,2,1:T(8,128)(2,1)}, f32[8,13,13,128]{3,0,2,1:T(8,128)}) fusion(f32[128]{0:T(128)S(1)} %get-tuple-element.26, bf16[8,13,13,512]{3,0,2,1:T(8,128)(2,1)} %all-gather.4.cloned.1.call-done, bf16[512,3,3,128]{3,2,1,0:T(4,128)(2,1)} %reshape_squeeze.6), kind=kOutput, calls=%fused_computation.105 | convolution fusion | flops 1437231104 | bytes 3602944 | tf_op jit(solution)/shard_map/conv_general_dilated | solution.py:39
  90.7 0.0 all-gather.8.cloned.1.call-update
  90.7 0.0 copy-start.7
  90.7 0.0 reduce-scatter.3.cloned.1.call-start
  90.8 0.6 reshape_squeeze.7
  91.4 18.2 %all-gather.8.cloned.1.call-done = bf16[8,13,13,512]{3,0,2,1:T(8,128)(2,1)} async-done(((bf16[8,13,13,128]{3,0,2,1:T(8,128)(2,1)}), bf16[8,13,13,512]{3,0,2,1:T(8,128)(2,1)}) %all-gather.8.cloned.1.call-update) | async-done | bytes 1384464 | tf_op jit(solution)/shard_map/all_gather | solution.py:82
  109.6 0.0 copy-done.7
  109.6 5.8 %convert_reduce_fusion.1 = (f32[128]{0:T(128)S(1)}, bf16[8,13,13,128]{3,0,2,1:T(8,128)(2,1)S(1)}, bf16[8,13,13,128]{3,0,2,1:T(8,128)(2,1)}) fusion(f32[8]{0:T(128)S(1)} %convert_element_type.37, bf16[8,13,13,128]{3,0,2,1:T(8,128)(2,1)S(1)} %copy-done.7, f32[128]{0:T(128)S(1)} %get-tuple-element.25, ...), kind=kOutput, calls=%fused_computation.102 | convolution fusion | flops 1440345984 | bytes 3603488 | tf_op jit(solution)/shard_map/conv_general_dilated | solution.py:39
  115.4 3.5 %fusion.54 = f32[8,13,13,512]{3,0,2,1:T(8,128)} fusion(bf16[8,13,13,128]{3,0,2,1:T(8,128)(2,1)S(1)} %get-tuple-element.21, bf16[512,3,3,128]{3,2,1,0:T(4,128)(2,1)S(1)} %reshape_squeeze.7), kind=kOutput, calls=%fused_computation.82 | convolution fusion | flops 1435500544 | bytes 4294656 | tf_op jit(solution)/shard_map/conv_general_dilated | solution.py:39
  118.9 0.0 reduce-scatter.3.cloned.1.call-update
  119.0 0.2 reduce-scatter.5.cloned.1.call-start
  119.2 1.1 copy-done.6
  120.3 0.7 fusion.35
  121.0 0.7 fusion.33
  121.7 0.7 fusion.31
  122.4 0.7 fusion.29
  123.1 0.7 fusion.53
  123.9 0.7 fusion.27
  124.6 0.7 fusion.25
  125.3 0.7 fusion.23
  126.0 0.7 fusion.21
  126.7 0.9 copy.105
  127.5 0.8 stack.117
  128.3 26.3 %reduce-scatter.3.cloned.1.call-done = f32[8,13,13,128]{3,0,2,1:T(8,128)} async-done(((f32[8,13,13,512]{3,0,2,1:T(8,128)}), f32[8,13,13,128]{3,0,2,1:T(8,128)}) %reduce-scatter.3.cloned.1.call-update) | async-done | bytes 692240 | tf_op jit(solution)/shard_map/reduce_scatter | solution.py:86
  154.7 1.8 convert_reduce_fusion.2
  156.5 3.5 %fusion.57 = f32[8,13,13,512]{3,0,2,1:T(8,128)} fusion(bf16[8,13,13,128]{3,0,2,1:T(8,128)(2,1)S(1)} %get-tuple-element.19, bf16[512,3,3,128]{3,2,1,0:T(4,128)(2,1)S(1)} %copy-done.1), kind=kOutput, calls=%fused_computation.85 | convolution fusion | flops 1435500544 | bytes 4294656 | tf_op jit(solution)/shard_map/conv_general_dilated | solution.py:39
  160.0 0.0 reduce-scatter.5.cloned.1.call-update
  160.1 1.3 copy-done.2
  161.4 0.7 fusion.51
  162.0 0.7 fusion.49
  162.8 0.7 fusion.47
  163.5 0.7 fusion.45
  164.2 0.7 fusion.19
  164.9 0.7 fusion.43
  165.6 0.7 fusion.41
  166.3 0.7 fusion.39
  167.0 0.7 fusion.37
  167.7 0.9 copy.104
  168.6 1.4 stack.106
  169.9 1.5 maximum_bitcast_fusion
  171.5 1.6 copy.106
  173.0 5.5 %all-to-all-start = ((bf16[8,2,576,128]{3,2,1,0:T(8,128)(2,1)}), bf16[8,2,576,128]{3,2,1,0:T(8,128)(2,1)S(1)}, u32[]{:S(2)}, u32[]{:S(2)}) async-start(bf16[8,2,576,128]{3,2,1,0:T(8,128)(2,1)} %copy.106), calls=%async_computation.2 | async-start | bytes 4718592 | tf_op jit(solution)/shard_map/all_to_all | solution.py:25
  178.6 0.0 copy-start.4
  178.6 0.0 copy-start.5
  178.6 0.0 copy-start
  178.6 53.8 %all-to-all-done = bf16[8,2,576,128]{3,2,1,0:T(8,128)(2,1)S(1)} async-done(((bf16[8,2,576,128]{3,2,1,0:T(8,128)(2,1)}), bf16[8,2,576,128]{3,2,1,0:T(8,128)(2,1)S(1)}, u32[]{:S(2)}, u32[]{:S(2)}) %all-to-all-start) | async-done | bytes 2359328 | tf_op jit(solution)/shard_map/all_to_all | solution.py:25
  232.4 0.3 convert_reduce_fusion
  232.8 0.8 multiply_reduce_fusion
  233.5 37.7 %all-reduce.2 = (f32[]{:T(128)}, f32[2,512]{1,0:T(2,128)S(1)}) all-reduce(f32[]{:T(128)} %multiply_reduce_fusion, f32[2,512]{1,0:T(2,128)S(1)} %maximum_dynamic-update-slice_fusion), channel_id=1, replica_groups=mesh['dp'=8,'tensor'=4] {'dp','tensor'}, use_global_device_ids=true, to_apply=%region_4.5 | all-reduce | flops 1025 | bytes 8200 | tf_op jit(solution)/shard_map/psum | solution.py:142
  271.2 0.6 multiply_reduce_fusion.1
  273.2 0.6 multiply_subtract_fusion.1
  273.9 2.8 multiply_subtract_fusion
  (15 shorter events, 0.1 us)
Async XLA Ops:
  7.2 2.7 copy-start.3
  7.2 58.4 %all-gather.6.cloned.1.call-start = ((), (), s32[]{:S(2)}) async-start(), calls=%async_computation.4 | async-start | bytes 2654208 | tf_op jit(solution)/shard_map/all_gather | solution.py:108
  9.1 75.4 %all-gather.4.cloned.1.call-start = ((), (), s32[]{:S(2)}) async-start(), calls=%async_computation.3 | async-start | bytes 1730560 | tf_op jit(solution)/shard_map/all_gather | solution.py:82
  9.8 99.8 %all-gather.8.cloned.1.call-start = ((), (), s32[]{:S(2)}) async-start(), calls=%async_computation.5 | async-start | bytes 1730560 | tf_op jit(solution)/shard_map/all_gather | solution.py:82
  84.5 6.3 %copy-start.8 = (s32[8]{0:T(128)S(1)}, s32[8]{0:T(128)}, u32[]{:S(2)}) copy-start(s32[8]{0:T(128)} %param.10) | copy-start | bytes 100
  90.7 18.9 %copy-start.7 = (bf16[8,13,13,128]{3,0,2,1:T(8,128)(2,1)S(1)}, bf16[8,13,13,128]{3,0,2,1:T(8,128)(2,1)}, u32[]{:S(2)}) copy-start(bf16[8,13,13,128]{3,0,2,1:T(8,128)(2,1)} %param.13) | copy-start | bytes 1038340
  90.7 64.0 %reduce-scatter.3.cloned.1.call-start = ((), (), s32[]{:S(2)}) async-start(), calls=%async_computation.6 | async-start | bytes 3461120 | tf_op jit(solution)/shard_map/reduce_scatter | solution.py:86
  118.9 1.3 copy-start.6
  119.0 157.7 %reduce-scatter.5.cloned.1.call-start = ((), (), s32[]{:S(2)}) async-start(), calls=%async_computation.7 | async-start | bytes 3461120 | tf_op jit(solution)/shard_map/reduce_scatter | solution.py:86
  128.3 28.2 %copy-start.1 = (bf16[512,3,3,128]{3,2,1,0:T(4,128)(2,1)S(1)}, bf16[512,3,3,128]{3,2,1,0:T(4,128)(2,1)}, u32[]{:S(2)}) copy-start(bf16[512,3,3,128]{3,2,1,0:T(4,128)(2,1)} %reshape_squeeze.6) | copy-start | bytes 3538948
  160.0 1.3 copy-start.2
  173.0 59.4 %all-to-all-start = ((bf16[8,2,576,128]{3,2,1,0:T(8,128)(2,1)}), bf16[8,2,576,128]{3,2,1,0:T(8,128)(2,1)S(1)}, u32[]{:S(2)}, u32[]{:S(2)}) async-start(bf16[8,2,576,128]{3,2,1,0:T(8,128)(2,1)} %copy.106), calls=%async_computation.2 | async-start | bytes 4718592 | tf_op jit(solution)/shard_map/all_to_all | solution.py:25
  178.6 94.6 %copy-start.4 = (f32[2,512]{1,0:T(2,128)S(1)}, f32[2,512]{1,0:T(2,128)}, u32[]{:S(2)}) copy-start(f32[2,512]{1,0:T(2,128)} %param.16) | copy-start | bytes 12292
  178.6 94.6 %copy-start.5 = (f32[2,512]{1,0:T(2,128)S(1)}, f32[2,512]{1,0:T(2,128)}, u32[]{:S(2)}) copy-start(f32[2,512]{1,0:T(2,128)} %param.17) | copy-start | bytes 12292
  178.6 95.2 %copy-start = (f32[2,576,128]{2,1,0:T(8,128)S(1)}, f32[2,576,128]{2,1,0:T(8,128)}, u32[]{:S(2)}) copy-start(f32[2,576,128]{2,1,0:T(8,128)} %param.11) | copy-start | bytes 1769476
Sparse Core Ops, SparseCore 0:
  10.8 54.7 all-gather.5
  67.2 17.2 all-gather.3
  90.8 18.7 all-gather.7
  119.1 35.5 reduce-scatter.2
  160.2 35.5 reduce-scatter.4
where the time goes:
time: 285 us; the launch traced here: 284 us
  waiting for transfers between devices  170 us (60%)
  blocking collectives  37.7 us (13%)
  matrix products  31.7 us (11%)
  between operations  16.5 us (6%)
  local copies, waits for them, and re-layouts  12.3 us (4%)
  other arithmetic  10.3 us (4%)
  starting transfers between devices  5.91 us (2%)
    all_gather x1, waiting for transfers between devices, on_device(): lax.all_gather(weights.astype(jnp.bfloat16), 'dp', axis=1, tiled=True)  55.7 us
    all_to_all x1, waiting for transfers between devices, sent_and_summed(): lax.all_to_all(parts, axis, split_axis=0, concat_axis=0, tiled=True)  53.8 us
    psum x1, blocking collectives, on_device(): lax.psum((placed, jnp.sum(grad_shard * grad_shard)), ('dp', 'tensor'))  37.7 us
    all_gather x2, waiting for transfers between devices, gather_channels(): return lax.all_gather(acts, 'tensor', axis=3, tiled=True)  33.4 us
    reduce_scatter x2, waiting for transfers between devices, sum_channels(): lax.psum_scatter(partial_sum, 'tensor', scatter_dimension=3, tiled=True)  26.3 us
    conv_general_dilated x4, matrix products, convolve(): lax.conv_general_dilated(inputs, kernel, (1, 1), ((1, 1), (1, 1)), dimens...  19.1 us
    dot_general x18, matrix products, kernel_grad(): lax.dot_general(shifted, flat_deltas, (((0,), (0,)), ((), ())), preferred...  12.6 us
  transfers between devices with their start and end apart: 6, of which 5 were waited for; matrix products, arithmetic and copies ran while one was open for 10% of the time, Pallas kernels for 0%

commit v1 on v0

v1 whole, which is shorter than its diff:
```python
import functools
import math

import jax
import jax.numpy as jnp
from jax import lax
from jax.experimental import pallas as pl
from jax.experimental.pallas import tpu as pltpu
from jax.sharding import PartitionSpec as P

STEP = 5
CLIP_NORM = 1.0
BETA_ONE = 0.5
BETA_TWO = 0.5
RATE = 0.01
BIAS_RATE = 0.03
DECAY = 0.1
EPSILON = 1e-08

MESH = pl.DeviceIdType.MESH
BF16 = jnp.bfloat16
F32 = jnp.float32
ROOT = math.sqrt(2.0 / math.pi)
CUBE = 0.044715
TAPS = 9
LANES = 128
PAD = 16
HALVES = 2
WIDE = 256


def gelu_parts(value):
    square = value * value
    th = jnp.tanh(ROOT * value * (1.0 + CUBE * square))
    half = 0.5 * (1.0 + th)
    slope = half + 0.5 * value * (1.0 - th * th) * (ROOT * (1.0 + 3.0 * CUBE * square))
    return value * half, slope


def flip_bits(index, mask):
    bit = 1
    while bit <= mask:
        if mask & bit:
            index = index + bit - 2 * bit * lax.rem(lax.div(index, bit), 2)
        bit *= 2
    return index


class Sizes:
    def __init__(self, mesh, frames_shape, weights_shape):
        self.dp = mesh.shape["dp"]
        self.tensor = mesh.shape["tensor"]
        self.items, self.height, self.width, self.out = frames_shape
        self.chan = self.out * self.tensor
        self.rows = weights_shape[1]
        self.own_in = self.rows // TAPS
        self.cols = TAPS * self.out
        self.major = self.dp // 2
        self.pairs = self.tensor // 2
        self.slots = self.dp // self.tensor
        self.spots = self.height * self.width
        self.span = -(-self.spots // 16) * 16
        self.wire = BF16 if self.own_in % 16 == 0 else F32
        self.group = self.items // HALVES


def body(
    sz,
    frames_ref,
    mask_ref,
    weights_ref,
    biases_ref,
    cot_ref,
    act4_out,
    act5_out,
    igrad_out,
    grads_out,
    stats_out,
    w_in,
    cot,
    w_all,
    frames,
    acts,
    spread,
    edges,
    slope4,
    act5,
    shifted,
    deltas,
    part_send,
    part_recv,
    part_own,
    cross_send,
    cross_recv,
    igrad,
    kgrad,
    near_send,
    near_recv,
    far_send,
    far_recv,
    shard,
    rows_out,
    bias_sum,
    stats_dp,
    stats_t,
    local_sem,
    out_sem,
    wz_send,
    wz_recv,
    wy_send,
    wy_recv,
    ax_send,
    ax_recv,
    as_send,
    as_recv,
    af_send,
    af_recv,
    rs_send,
    rs_recv,
    rx_send,
    rx_recv,
    gy_send,
    gy_recv,
    gz_send,
    gz_recv,
    sd_send,
    sd_recv,
    st_send,
    st_recv,
):
    d = lax.axis_index("dp")
    t = lax.axis_index("tensor")
    major, minor = lax.div(d, 2), lax.rem(d, 2)
    near = (2 * major + 1 - minor, t)
    pair, side = lax.div(t, 2), lax.rem(t, 2)
    sibling = (d, 2 * pair + 1 - side)

    def far_slot(k):
        return 2 * flip_bits(major, k) + minor

    def far(k):
        return (far_slot(k), t)

    def cross_rank(k):
        return 2 * lax.rem(pair + k, sz.pairs) + side

    def cross_from(k):
        return 2 * lax.rem(pair + sz.pairs - k, sz.pairs) + side

    def remote(src, dst, send, recv, device):
        return pltpu.make_async_remote_copy(
            src_ref=src, dst_ref=dst, send_sem=send, recv_sem=recv, device_id=device, device_id_type=MESH
        )

    far_steps = range(1, sz.major)
    cross_steps = range(1, sz.pairs)
    group = sz.group

    load_w = [pltpu.make_async_copy(weights_ref.at[l], w_in.at[l], local_sem.at[l]) for l in (0, 1)]
    load_frames = pltpu.make_async_copy(frames_ref, frames.at[t], local_sem.at[2])
    load_cot = pltpu.make_async_copy(cot_ref, cot, local_sem.at[3])
    load_w[0].start()
    load_frames.start()
    load_w[1].start()
    load_cot.start()

    barrier = pltpu.get_barrier_semaphore()
    for k in range(1, sz.dp):
        pl.semaphore_signal(barrier, inc=1, device_id=(lax.rem(d + k, sz.dp), t), device_id_type=MESH)
    for k in range(1, sz.tensor):
        pl.semaphore_signal(barrier, inc=1, device_id=(d, lax.rem(t + k, sz.tensor)), device_id_type=MESH)

    rest = sz.span + PAD
    for edge in (slice(0, PAD), slice(rest, rest + PAD)):
        spread[:, edge, :] = jnp.zeros((group, PAD, sz.cols), F32)
        shifted[:, edge, :] = jnp.zeros((3, PAD, sz.out), F32)
    spot = lax.broadcasted_iota(jnp.int32, (sz.span, sz.out), 0)
    column = lax.rem(spot, sz.width)
    edges[0] = (column > 0).astype(F32)
    edges[1] = (column < sz.width - 1).astype(F32)
    edges[2] = (spot < sz.spots).astype(F32)
    bias_sum[...] = jnp.zeros_like(bias_sum)

    def weight_sends(l):
        out = [remote(w_all.at[l, d], w_all.at[l, d], wz_send.at[l, k], wz_recv.at[l, k], far(k)) for k in far_steps]
        out.append(remote(w_all.at[l, d], w_all.at[l, d], wy_send.at[l, 0], wy_recv.at[l, 0], near))
        return out

    def weight_forward(l, k):
        slot = far_slot(k)
        return remote(w_all.at[l, slot], w_all.at[l, slot], wy_send.at[l, k], wy_recv.at[l, k], near)

    def weight_from_far(l, k):
        slot = far_slot(k)
        remote(w_all.at[l, slot], w_all.at[l, slot], wz_send.at[l, k], wz_recv.at[l, k], far(k)).wait_recv()

    def weight_from_near(l, k):
        slot = 2 * flip_bits(major, k) + 1 - minor
        remote(w_all.at[l, slot], w_all.at[l, slot], wy_send.at[l, k], wy_recv.at[l, k], near).wait_recv()

    def round_weights(l):
        load_w[l].wait()
        for tap in range(TAPS):
            w_all[l, d, :, tap * sz.out : (tap + 1) * sz.out] = w_in[
                l, pl.ds(tap, sz.own_in, stride=TAPS), :
            ].astype(sz.wire)

    pl.semaphore_wait(barrier, sz.dp + sz.tensor - 2)

    round_weights(0)
    sends = weight_sends(0)
    for copy in sends:
        copy.start()

    def piece(maps, rank, h):
        return maps.at[rank, pl.ds(h * group, group)]

    def gather_sends(g, maps, h):
        own = piece(maps, t, h)
        out = [remote(own, own, ax_send.at[g, h, k], ax_recv.at[g, h, k], (d, cross_rank(k))) for k in cross_steps]
        out.append(remote(own, own, as_send.at[g, h], as_recv.at[g, h], sibling))
        return out

    def gather_forward(g, maps, h, k):
        block = piece(maps, cross_from(k), h)
        return remote(block, block, af_send.at[g, h, k], af_recv.at[g, h, k], sibling)

    def gather_from_cross(g, maps, h, k):
        block = piece(maps, cross_from(k), h)
        remote(block, block, ax_send.at[g, h, k], ax_recv.at[g, h, k], sibling).wait_recv()

    def gather_from_sibling(g, maps, h):
        block = piece(maps, sibling[1], h)
        remote(block, block, as_send.at[g, h], as_recv.at[g, h], sibling).wait_recv()
        for k in cross_steps:
            rank = 2 * lax.rem(pair + sz.pairs - k, sz.pairs) + 1 - side
            block = piece(maps, rank, h)
            remote(block, block, af_send.at[g, h, k], af_recv.at[g, h, k], sibling).wait_recv()

    def gather_all(g, maps):
        for h in range(HALVES):
            for k in cross_steps:
                gather_from_cross(g, maps, h, k)
                gather_forward(g, maps, h, k).start()
        for h in range(HALVES):
            gather_from_sibling(g, maps, h)

    def gather_sent(g, maps):
        for h in range(HALVES):
            for copy in gather_sends(g, maps, h):
                copy.wait_send()
            for k in cross_steps:
                gather_forward(g, maps, h, k).wait_send()

    load_frames.wait()
    for h in range(HALVES):
        for copy in gather_sends(0, frames, h):
            copy.start()
    round_weights(1)
    gather_all(0, frames)

    for k in far_steps:
        weight_from_far(0, k)
        weight_forward(0, k).start()
    sends = weight_sends(1)
    for copy in sends:
        copy.start()
    for k in range(sz.major):
        weight_from_near(0, k)

    def convolve(l, maps, finish, after):
        @pl.loop(0, HALVES)
        def _(h):
            left = jnp.concatenate(
                [maps[q, pl.ds(h * group, group)].reshape(group * sz.span, sz.out) for q in range(sz.tensor)], axis=1
            )
            for start in range(0, sz.cols, WIDE):
                stop = min(start + WIDE, sz.cols)
                right = w_all[l, :, :, start:stop].reshape(sz.chan, stop - start).astype(BF16)
                product = jnp.dot(left, right, preferred_element_type=F32)
                spread[:, PAD:rest, start:stop] = product.reshape(group, sz.span, stop - start)

            @pl.loop(0, group)
            def _(m):
                sums = []
                for b in range(3):
                    total = None
                    for a in range(3):
                        first = PAD + sz.width * (a - 1) + b - 1
                        tap = 3 * a + b
                        term = spread[m, pl.ds(first, sz.span), tap * sz.out : (tap + 1) * sz.out]
                        total = term if total is None else total + term
                    sums.append(total)
                finish(h * group + m, sums[1] + sums[0] * edges[0] + sums[2] * edges[1])

            after(h)

    def own_bias(l):
        return biases_ref[l : l + 1, pl.ds(pl.multiple_of(t * sz.out, sz.out), sz.out)]

    def finish_four(n, value):
        act, slope = gelu_parts(value + own_bias(0))
        acts[t, n] = (act * edges[2]).astype(BF16)
        slope4[n] = slope * edges[2]

    def after_four(h):
        for copy in gather_sends(1, acts, h):
            copy.start()

    convolve(0, frames, finish_four, after_four)
    save_act4 = pltpu.make_async_copy(acts.at[t], act4_out, out_sem.at[0])
    save_act4.start()

    for k in far_steps:
        weight_from_far(1, k)
        weight_forward(1, k).start()
    gather_all(1, acts)
    for k in range(sz.major):
        weight_from_near(1, k)

    def spread_delta(l, n, delta):
        bias_sum[l, :, :] += jnp.sum(delta.reshape(sz.span // 8, 8, sz.out), axis=0)
        shifted[0, PAD:rest, :] = delta * edges[0]
        shifted[1, PAD:rest, :] = delta
        shifted[2, PAD:rest, :] = delta * edges[1]
        for a in range(3):
            for b in range(3):
                first = PAD - sz.width * (a - 1) - (b - 1)
                tap = 3 * a + b
                deltas[n, :, tap * sz.out : (tap + 1) * sz.out] = shifted[b, pl.ds(first, sz.span), :].astype(BF16)

    load_cot.wait()

    def finish_five(n, value):
        act, slope = gelu_parts(value + own_bias(1))
        keep = mask_ref[n].astype(F32)
        act5[n] = (act * keep).astype(BF16)
        delta = (cot[n].astype(F32) * keep * slope).astype(BF16).astype(F32)
        spread_delta(1, n, delta)

    convolve(1, acts, finish_five, lambda h: None)
    save_act5 = pltpu.make_async_copy(act5, act5_out, out_sem.at[1])
    save_act5.start()

    def part_copy(l, h):
        own = part_send.at[l, :, pl.ds(h * group, group)]
        there = part_recv.at[l, :, pl.ds(h * group, group)]
        return remote(own, there, rs_send.at[l, h], rs_recv.at[l, h], sibling)

    def cross_copy(l, h, k):
        return remote(
            cross_send.at[l, k, pl.ds(h * group, group)],
            cross_recv.at[l, k, pl.ds(h * group, group)],
            rx_send.at[l, h, k],
            rx_recv.at[l, h, k],
            (d, cross_rank(k)),
        )

    def back_products(l):
        def weights_for(which):
            blocks = [
                w_all[l, pl.ds((2 * j + which) * sz.slots, sz.slots)].reshape(sz.out, sz.cols) for j in range(sz.pairs)
            ]
            return jnp.concatenate(blocks, axis=0).astype(BF16)

        def products(h, right):
            left = deltas[pl.ds(h * group, group)].reshape(group * sz.span, sz.cols)
            out = lax.dot_general(left, right, (((1,), (1,)), ((), ())), preferred_element_type=F32)
            return [out[:, j * sz.out : (j + 1) * sz.out].reshape(group, sz.span, sz.out) for j in range(sz.pairs)]

        @pl.loop(0, HALVES)
        def _(h):
            for j, block in enumerate(products(h, weights_for(1 - side))):
                part_send[l, j, pl.ds(h * group, group)] = block.astype(BF16)
            part_copy(l, h).start()

        @pl.loop(0, HALVES)
        def _(h):
            for j, block in enumerate(products(h, weights_for(side))):
                part_own[j, pl.ds(h * group, group)] = block

        for h in range(HALVES):
            part_copy(l, h).wait_recv()
            items = pl.ds(h * group, group)
            for k in cross_steps:
                j = lax.rem(pair + k, sz.pairs)
                cross_send[l, k, items] = (part_own[j, items] + part_recv[l, j, items].astype(F32)).astype(BF16)
                cross_copy(l, h, k).start()

    def back_total(l, n):
        total = part_own[pair, n] + part_recv[l, pair, n].astype(F32)
        for k in cross_steps:
            total += cross_recv[l, k, n].astype(F32)
        return total

    def near_copy(l, k):
        return remote(near_send.at[l, k], near_recv.at[l, k], gy_send.at[l, k], gy_recv.at[l, k], near)

    def far_copy(l, k):
        return remote(far_send.at[l, k], far_recv.at[l, k], gz_send.at[l, k], gz_recv.at[l, k], far(k))

    grad_order = [*reversed(far_steps), 0]

    def weight_grads(l, maps):
        left = jnp.concatenate([maps[q].reshape(sz.items * sz.span, sz.out) for q in range(sz.tensor)], axis=1)
        for start in range(0, sz.cols, WIDE):
            stop = min(start + WIDE, sz.cols)
            right = deltas[:, :, start:stop].reshape(sz.items * sz.span, stop - start)
            product = lax.dot_general(left, right, (((0,), (0,)), ((), ())), preferred_element_type=F32)
            kgrad[l, :, :, start:stop] = product.reshape(sz.dp, sz.own_in, stop - start)
        for k in grad_order:
            near_send[l, k] = kgrad[l, 2 * flip_bits(major, k) + 1 - minor].astype(sz.wire)
            near_copy(l, k).start()

    def grads_to_far(l):
        for k in grad_order:
            near_copy(l, k).wait_recv()
            if k:
                far_send[l, k] = (kgrad[l, far_slot(k)] + near_recv[l, k].astype(F32)).astype(sz.wire)
                far_copy(l, k).start()

    def grads_done(l):
        total = kgrad[l, d] + near_recv[l, 0].astype(F32)
        for k in far_steps:
            far_copy(l, k).wait_recv()
            total += far_recv[l, k].astype(F32)
        shard[...] = total
        squares = jnp.sum((total * total).reshape(sz.own_in // 8, 8, sz.cols), axis=0)
        for tap in range(TAPS):
            rows_out[l, pl.ds(tap, sz.own_in, stride=TAPS), :] = shard[:, tap * sz.out : (tap + 1) * sz.out]
        return sum(squares[:, tap * sz.out : (tap + 1) * sz.out] for tap in range(TAPS))

    back_products(1)
    weight_grads(1, acts)

    for h in range(HALVES):
        for k in cross_steps:
            cross_copy(1, h, k).wait_recv()

        @pl.loop(h * group, (h + 1) * group)
        def _(n):
            delta = (back_total(1, n) * slope4[n]).astype(BF16).astype(F32)
            spread_delta(0, n, delta)

    weight_grads(0, frames)
    grads_to_far(1)
    back_products(0)
    grads_to_far(0)

    for h in range(HALVES):
        for k in cross_steps:
            cross_copy(0, h, k).wait_recv()

        @pl.loop(h * group, (h + 1) * group)
        def _(n):
            igrad[n] = back_total(0, n)

    save_igrad = pltpu.make_async_copy(igrad, igrad_out, out_sem.at[2])
    save_igrad.start()

    squares = grads_done(1)
    save_grads = [pltpu.make_async_copy(rows_out.at[l], grads_out.at[l], out_sem.at[3 + l]) for l in (0, 1)]
    save_grads[1].start()
    squares += grads_done(0)
    save_grads[0].start()

    stats_dp[d, 0:1, :] = jnp.sum(squares, axis=0, keepdims=True)
    for l in (0, 1):
        stats_dp[d, l + 1 : l + 2, :] = jnp.sum(bias_sum[l], axis=0, keepdims=True)
    stats_dp[d, 3:8, :] = jnp.zeros((5, sz.out), F32)

    def stats_over_dp(k, slot):
        return remote(
            stats_dp.at[slot], stats_dp.at[slot], sd_send.at[k], sd_recv.at[k], (lax.rem(d + k, sz.dp), t)
        )

    def stats_over_tensor(k, slot):
        return remote(
            stats_t.at[slot], stats_t.at[slot], st_send.at[k], st_recv.at[k], (d, lax.rem(t + k, sz.tensor))
        )

    for k in range(1, sz.dp):
        stats_over_dp(k, d).start()
    for k in range(1, sz.dp):
        stats_over_dp(k, lax.rem(d + sz.dp - k, sz.dp)).wait_recv()
    total = stats_dp[0]
    for slot in range(1, sz.dp):
        total += stats_dp[slot]
    stats_t[t] = total
    for k in range(1, sz.tensor):
        stats_over_tensor(k, t).start()
    for k in range(1, sz.tensor):
        stats_over_tensor(k, lax.rem(t + sz.tensor - k, sz.tensor)).wait_recv()
    save_stats = pltpu.make_async_copy(stats_t, stats_out, out_sem.at[5])
    save_stats.start()

    for l in (0, 1):
        for copy in weight_sends(l):
            copy.wait_send()
        for k in far_steps:
            weight_forward(l, k).wait_send()
            far_copy(l, k).wait_send()
        for k in range(sz.major):
            near_copy(l, k).wait_send()
        for h in range(HALVES):
            part_copy(l, h).wait_send()
            for k in cross_steps:
                cross_copy(l, h, k).wait_send()
    gather_sent(0, frames)
    gather_sent(1, acts)
    for k in range(1, sz.dp):
        stats_over_dp(k, d).wait_send()
    for k in range(1, sz.tensor):
        stats_over_tensor(k, t).wait_send()
    for copy in (save_act4, save_act5, save_igrad, *save_grads, save_stats):
        copy.wait()


def train_step(sz, frames, item_mask, weights, biases, cotangent):
    sem = pltpu.SemaphoreType.DMA
    vmem = pltpu.VMEM
    maps = (sz.items, sz.span, sz.out)
    shapes = [
        vmem((2, sz.rows, sz.out), F32),
        vmem(maps, BF16),
        vmem((2, sz.dp, sz.own_in, sz.cols), sz.wire),
        vmem((sz.tensor, *maps), BF16),
        vmem((sz.tensor, *maps), BF16),
        vmem((sz.group, sz.span + 2 * PAD, sz.cols), F32),
        vmem((3, sz.span, sz.out), F32),
        vmem(maps, F32),
        vmem(maps, BF16),
        vmem((3, sz.span + 2 * PAD, sz.out), F32),
        vmem((sz.items, sz.span, sz.cols), BF16),
        vmem((2, sz.pairs, *maps), BF16),
        vmem((2, sz.pairs, *maps), BF16),
        vmem((sz.pairs, *maps), F32),
        vmem((2, sz.pairs, *maps), BF16),
        vmem((2, sz.pairs, *maps), BF16),
        vmem(maps, F32),
        vmem((2, sz.dp, sz.own_in, sz.cols), F32),
        vmem((2, sz.major, sz.own_in, sz.cols), sz.wire),
        vmem((2, sz.major, sz.own_in, sz.cols), sz.wire),
        vmem((2, sz.major, sz.own_in, sz.cols), sz.wire),
        vmem((2, sz.major, sz.own_in, sz.cols), sz.wire),
        vmem((sz.own_in, sz.cols), F32),
        vmem((2, sz.rows, sz.out), F32),
        vmem((2, 8, sz.out), F32),
        vmem((sz.dp, 8, sz.out), F32),
        vmem((sz.tensor, 8, sz.out), F32),
        sem((4,)),
        sem((6,)),
        sem((2, sz.major)),
        sem((2, sz.major)),
        sem((2, sz.major)),
        sem((2, sz.major)),
        sem((2, HALVES, sz.pairs)),
        sem((2, HALVES, sz.pairs)),
        sem((2, HALVES)),
        sem((2, HALVES)),
        sem((2, HALVES, sz.pairs)),
        sem((2, HALVES, sz.pairs)),
        sem((2, HALVES)),
        sem((2, HALVES)),
        sem((2, HALVES, sz.pairs)),
        sem((2, HALVES, sz.pairs)),
        sem((2, sz.major)),
        sem((2, sz.major)),
        sem((2, sz.major)),
        sem((2, sz.major)),
        sem((sz.dp,)),
        sem((sz.dp,)),
        sem((sz.tensor,)),
        sem((sz.tensor,)),
    ]
    anywhere = pl.BlockSpec(memory_space=pl.ANY)
    macs = 6 * sz.items * sz.spots * TAPS * sz.chan * sz.out
    return pl.pallas_call(
        functools.partial(body, sz),
        out_shape=[
            jax.ShapeDtypeStruct(maps, BF16),
            jax.ShapeDtypeStruct(maps, BF16),
            jax.ShapeDtypeStruct(maps, F32),
            jax.ShapeDtypeStruct((2, sz.rows, sz.out), F32),
            jax.ShapeDtypeStruct((sz.tensor, 8, sz.out), F32),
        ],
        in_specs=[
            anywhere,
            pl.BlockSpec(memory_space=pltpu.SMEM),
            anywhere,
            pl.BlockSpec(memory_space=pltpu.VMEM),
            anywhere,
        ],
        out_specs=[anywhere] * 5,
        scratch_shapes=shapes,
        compiler_params=pltpu.CompilerParams(
            collective_id=0, has_side_effects=True, vmem_limit_bytes=58 * 1024 * 1024
        ),
        cost_estimate=pl.CostEstimate(flops=2 * macs, bytes_accessed=6_000_000, transcendentals=0),
        name="train_step",
    )(frames, item_mask, weights, biases, cotangent)


def adam_update(param, grad, first, second, rate, decay):
    first_new = BETA_ONE * first + (1.0 - BETA_ONE) * grad
    second_new = BETA_TWO * second + (1.0 - BETA_TWO) * grad * grad
    corrected = first_new / (1.0 - BETA_ONE**STEP)
    scaled = jnp.sqrt(second_new / (1.0 - BETA_TWO**STEP)) + EPSILON
    return (param - rate * (corrected / scaled + decay * param), first_new, second_new)


def on_device(
    mesh,
    frames,
    item_mask,
    weights,
    biases,
    cotangent,
    weight_first,
    weight_second,
    bias_first,
    bias_second,
):
    sz = Sizes(mesh, frames.shape, weights.shape)

    def flat(maps):
        rows = maps.reshape(sz.items, sz.spots, sz.out)
        return jnp.pad(rows, ((0, 0), (0, sz.span - sz.spots), (0, 0)))

    def square(rows):
        return rows[:, : sz.spots].reshape(sz.items, sz.height, sz.width, sz.out)

    act_four, act_five, input_grad, grad_shard, stats = train_step(
        sz, flat(frames), item_mask, weights, biases, flat(cotangent)
    )
    bias_grad = jnp.moveaxis(stats[:, 1:3, :], 1, 0).reshape(2, sz.chan)
    grad_norm = jnp.sqrt(jnp.sum(stats[:, 0, :]) + jnp.sum(bias_grad * bias_grad))
    factor = jnp.minimum(1.0, CLIP_NORM / (grad_norm + 1e-06))
    new_weights, weight_m, weight_v = adam_update(
        weights, grad_shard * factor, weight_first, weight_second, RATE, DECAY
    )
    new_biases, bias_m, bias_v = adam_update(
        biases, bias_grad * factor, bias_first, bias_second, BIAS_RATE, 0.0
    )
    return (
        square(act_four),
        square(act_five),
        square(input_grad),
        grad_norm,
        new_weights,
        weight_m,
        weight_v,
        new_biases,
        bias_m,
        bias_v,
    )


def solution(mesh):
    split = P("dp", None, None, "tensor")
    rows = P(None, "dp", "tensor")
    in_specs = (split, P("dp"), rows, P(), split, rows, rows, P(), P())
    out_specs = (split, split, split, P(), rows, rows, rows, P(), P(), P())
    return jax.shard_map(
        functools.partial(on_device, mesh), mesh=mesh, in_specs=in_specs, out_specs=out_specs, check_vma=False
    )
```

time: 285 us -> 116 us (0.41)
  waiting for transfers between devices: 170 us -> 0 us
  Pallas kernels: 0 us -> 98.8 us
  blocking collectives: 37.7 us -> 0 us
  matrix products: 31.7 us -> 0 us
  between operations: 16.5 us -> 3.23 us
  starting transfers between devices: 5.91 us -> 0 us
  local copies, waits for them, and re-layouts: 12.3 us -> 7.16 us
  other arithmetic: 10.3 us -> 6.59 us
    pallas_call x0 -> x1, Pallas kernels: none -> 98.8 us  [train_step(): pl.pallas_call(functools.partial(body, sz), out_shape=[jax.ShapeDtypeStru...]
    all_gather x3 -> x0, waiting for transfers between devices: 89.1 us -> none  [the longest x1 55.7 us: on_device(): lax.all_gather(weights.astype(jnp.bfloat16), 'dp', axis=1, tiled=True)]
    all_to_all x1 -> x0, waiting for transfers between devices: 53.8 us -> none  [sent_and_summed(): lax.all_to_all(parts, axis, split_axis=0, concat_axis=0, tiled=True)]
    psum x1 -> x0, blocking collectives: 37.7 us -> none  [on_device(): lax.psum((placed, jnp.sum(grad_shard * grad_shard)), ('dp', 'tensor'))]
    reduce_scatter x2 -> x0, waiting for transfers between devices: 26.3 us -> none  [sum_channels(): lax.psum_scatter(partial_sum, 'tensor', scatter_dimension=3, tiled=True)]
    conv_general_dilated x4 -> x0, matrix products: 19.1 us -> none  [convolve(): lax.conv_general_dilated(inputs, kernel, (1, 1), ((1, 1), (1, 1)), dimens...]
    dot_general x18 -> x0, matrix products: 12.6 us -> none  [kernel_grad(): lax.dot_general(shifted, flat_deltas, (((0,), (0,)), ((), ())), preferred...]
    another operation x7 -> x0, local copies, waits for them, and re-layouts: 6.44 us -> none  [the longest x2 2.55 us: to_kernel(): weight_rows.reshape(in_chan, 3, 3, weight_rows.shape[1])]
  transfers between devices with their start and end apart: 6 -> 0, of which waited for: 5 -> 0; matrix products, arithmetic and copies ran while one was open for 10% -> 0% of each run, Pallas kernels for 0% -> 0%
where the time goes in v1:
time: 116 us
  Pallas kernels  98.8 us (85%)
  local copies, waits for them, and re-layouts  7.16 us (6%)
  other arithmetic  6.59 us (6%)
  between operations  3.23 us (3%)
    pallas_call x1, Pallas kernels, train_step(): pl.pallas_call(functools.partial(body, sz), out_shape=[jax.ShapeDtypeStru...  98.8 us
    sub x2, other arithmetic, adam_update(): param - rate * (corrected / scaled + decay * param)  3.94 us
    slice x3, local copies, waits for them, and re-layouts, square(): return rows[:, :sz.spots].reshape(sz.items, sz.height, sz.width, sz.out)  3.77 us

profile of v1, /device:TPU:0, one launch (start us, length us, event | category | flops | bytes accessed | tf_op | source)
XLA Modules:
  0.0 115.8 jit_solution(4351104343877375884)
XLA Ops:
  0.6 1.0 copy.24
  1.7 0.0 copy-start.5
  1.7 0.8 pad.7.frames_ref
  2.5 0.3 copy-done.5
  2.8 0.1 copy.25
  2.8 0.8 pad.8.cot_ref
  3.6 98.8 %train_step.1 = (bf16[8,176,128]{2,1,0:T(8,128)(2,1)}, bf16[8,176,128]{2,1,0:T(8,128)(2,1)}, f32[8,176,128]{2,1,0:T(8,128)}, f32[2,576,128]{2,1,0:T(8,128)}, f32[4,8,128]{2,1,0:T(8,128)}) custom-call(bf16[8,176,128]{2,1,0:T(8,128)(2,1)} %pad.7.frames_ref, s32[8]{0:T(128)} %mask_ref.1, f32[2,576,128]{2,1,0:T(8,128)} %weights_ref.1, f32[2,512]{1,0:T(2,128)} %biases_ref.1, ...), custom_call_target="tpu_custom_call" | custom-call | flops 9569304576 | bytes 6000000 | tf_op jit(solution)/shard_map/train_step/pallas_call | solution.py:578
  102.4 1.3 %multiply_reduce_fusion = f32[]{:T(128)} fusion(f32[4,8,128]{2,1,0:T(8,128)} %get-tuple-element.18), kind=kLoop, calls=%fused_computation.8 | loop fusion | flops 2047 | bytes 4100 | tf_op jit(solution)/shard_map/reduce_sum | solution.py:637
  103.7 1.3 %slice_reduce_fusion = f32[]{:T(128)} fusion(f32[4,8,128]{2,1,0:T(8,128)} %get-tuple-element.18), kind=kLoop, calls=%fused_computation.9 | loop fusion | flops 511 | bytes 2052 | tf_op jit(solution)/shard_map/reduce_sum | solution.py:637
  106.4 0.0 copy-start.4
  106.4 0.0 copy-start.6
  106.4 0.0 copy-start.7
  106.5 0.0 copy-start.8
  106.5 0.0 copy-start
  106.5 1.9 %copy.26 = bf16[8,169,128]{2,0,1:T(8,128)(2,1)} copy(bf16[8,169,128]{2,1,0:T(8,128)(2,1)} %bitcast.18) | data formatting | bytes 692224 | tf_op jit(solution)/shard_map/slice | solution.py:631
  108.4 0.0 copy-done.4
  108.4 0.0 copy-start.3
  108.4 0.8 copy.27
  109.2 0.0 copy-done.6
  109.2 0.0 copy-done.7
  109.2 0.0 copy-done.8
  109.2 1.3 %multiply_subtract_fusion.1 = (f32[2,512]{1,0:T(2,128)}, f32[2,512]{1,0:T(2,128)}, f32[2,512]{1,0:T(2,128)}) fusion(f32[2,512]{1,0:T(2,128)S(1)} %copy-done.6, f32[]{:T(128)S(6)} %min.3, f32[4,8,128]{2,1,0:T(8,128)} %get-tuple-element.18, f32[2,512]{1,0:T(2,128)S(1)} %copy-done.7, f32[2,512]{1,0:T(2,128)S(1)} %copy-done.8), kind=kLoop, calls=%fused_computation.7 | loop fusion | flops 15360 | bytes 28676 | tf_op jit(solution)/shard_map/sub | solution.py:609
  110.5 0.0 copy-done
  110.5 0.0 copy-start.1
  110.5 0.0 copy-start.2
  110.5 1.1 copy.28
  111.6 0.0 copy-done.3
  111.6 0.0 copy-done.1
  111.6 0.4 copy-done.2
  112.0 2.6 %multiply_subtract_fusion = (f32[2,576,128]{2,1,0:T(8,128)}, f32[2,576,128]{2,1,0:T(8,128)}, f32[2,576,128]{2,1,0:T(8,128)}) fusion(f32[2,576,128]{2,1,0:T(8,128)S(1)} %copy-done.1, f32[2,576,128]{2,1,0:T(8,128)} %get-tuple-element.19, f32[]{:T(128)S(6)} %min.3, f32[2,576,128]{2,1,0:T(8,128)S(1)} %copy-done.2, f32[2,576,128]{2,1,0:T(8,128)S(1)} %copy-done.3), kind=kLoop, calls=%fused_computation.3 | loop fusion | flops 2211840 | bytes 4128772 | tf_op jit(solution)/shard_map/sub | solution.py:609
Async XLA Ops:
  1.7 1.1 copy-start.5
  106.4 1.9 %copy-start.4 = (bf16[8,176,128]{2,1,0:T(8,128)(2,1)S(1)}, bf16[8,176,128]{2,1,0:T(8,128)(2,1)}, u32[]{:S(2)}) copy-start(bf16[8,176,128]{2,1,0:T(8,128)(2,1)} %get-tuple-element.16) | copy-start | bytes 1081348
  106.4 2.8 %copy-start.6 = (f32[2,512]{1,0:T(2,128)S(1)}, f32[2,512]{1,0:T(2,128)}, u32[]{:S(2)}) copy-start(f32[2,512]{1,0:T(2,128)} %biases_ref.1) | copy-start | bytes 12292
  106.4 2.7 %copy-start.7 = (f32[2,512]{1,0:T(2,128)S(1)}, f32[2,512]{1,0:T(2,128)}, u32[]{:S(2)}) copy-start(f32[2,512]{1,0:T(2,128)} %param.16) | copy-start | bytes 12292
  106.5 2.7 %copy-start.8 = (f32[2,512]{1,0:T(2,128)S(1)}, f32[2,512]{1,0:T(2,128)}, u32[]{:S(2)}) copy-start(f32[2,512]{1,0:T(2,128)} %param.17) | copy-start | bytes 12292
  106.5 4.1 %copy-start = (f32[8,176,128]{2,1,0:T(8,128)S(1)}, f32[8,176,128]{2,1,0:T(8,128)}, u32[]{:S(2)}) copy-start(f32[8,176,128]{2,1,0:T(8,128)} %get-tuple-element.17) | copy-start | bytes 2162692
  108.4 3.2 %copy-start.3 = (f32[2,576,128]{2,1,0:T(8,128)S(1)}, f32[2,576,128]{2,1,0:T(8,128)}, u32[]{:S(2)}) copy-start(f32[2,576,128]{2,1,0:T(8,128)} %param.15) | copy-start | bytes 1769476
  110.5 1.1 copy-start.1
  110.5 1.5 %copy-start.2 = (f32[2,576,128]{2,1,0:T(8,128)S(1)}, f32[2,576,128]{2,1,0:T(8,128)}, u32[]{:S(2)}) copy-start(f32[2,576,128]{2,1,0:T(8,128)} %param.14) | copy-start | bytes 1769476

commit v2 on v1

v2 whole, which is shorter than its diff:
```python
import functools
import math

import jax
import jax.numpy as jnp
from jax import lax
from jax.experimental import pallas as pl
from jax.experimental.pallas import tpu as pltpu
from jax.sharding import PartitionSpec as P

STEP = 5
CLIP_NORM = 1.0
BETA_ONE = 0.5
BETA_TWO = 0.5
RATE = 0.01
BIAS_RATE = 0.03
DECAY = 0.1
EPSILON = 1e-08

MESH = pl.DeviceIdType.MESH
BF16 = jnp.bfloat16
F32 = jnp.float32
ROOT = math.sqrt(2.0 / math.pi)
CUBE = 0.044715
TAPS = 9
WIDE = 256


def gelu_parts(value):
    square = value * value
    th = jnp.tanh(ROOT * value * (1.0 + CUBE * square))
    half = 0.5 * (1.0 + th)
    slope = half + 0.5 * value * (1.0 - th * th) * (ROOT * (1.0 + 3.0 * CUBE * square))
    return value * half, slope


def flip_bits(index, mask):
    bit = 1
    while bit <= mask:
        if mask & bit:
            index = index + bit - 2 * bit * lax.rem(lax.div(index, bit), 2)
        bit *= 2
    return index


def adam_update(param, grad, first, second, rate, decay):
    first_new = BETA_ONE * first + (1.0 - BETA_ONE) * grad
    second_new = BETA_TWO * second + (1.0 - BETA_TWO) * grad * grad
    corrected = first_new / (1.0 - BETA_ONE**STEP)
    scaled = jnp.sqrt(second_new / (1.0 - BETA_TWO**STEP)) + EPSILON
    return (param - rate * (corrected / scaled + decay * param), first_new, second_new)


class Sizes:
    def __init__(self, mesh, frames_shape, weights_shape):
        self.dp = mesh.shape["dp"]
        self.tensor = mesh.shape["tensor"]
        self.items, self.height, self.width, self.out = frames_shape
        self.chan = self.out * self.tensor
        self.rows = weights_shape[1]
        self.own_in = self.rows // TAPS
        self.cols = TAPS * self.out
        self.major = self.dp // 2
        self.pairs = self.tensor // 2
        self.slots = self.dp // self.tensor
        self.spots = self.height * self.width
        self.real = self.spots * self.items
        self.span = -(-self.real // 16) * 16
        self.halo = (self.width + 1) * self.items
        self.pieces = next(n for n in (5, 4, 3, 2, 1) if self.span // 16 % n == 0)
        self.piece = self.span // self.pieces
        self.groups = ((0, self.pieces // 2), (self.pieces // 2, self.pieces))
        self.wire = BF16 if self.own_in % 16 == 0 else F32
        self.relay = self.major == 4
        self.far_order = (2, 1, 3) if self.relay else tuple(range(1, self.major))


def body(
    sz,
    frames_ref,
    mask_ref,
    weights_ref,
    biases_ref,
    cot_ref,
    act4_out,
    act5_out,
    igrad_out,
    grads_out,
    stats_out,
    w_in,
    stage,
    cot,
    biases,
    mask,
    keep,
    w_all,
    frames,
    acts,
    spread,
    edges,
    slope4,
    act5,
    shifted,
    deltas,
    part_send,
    part_recv,
    part_own,
    cross_send,
    cross_recv,
    igrad,
    kgrad,
    near_send,
    near_recv,
    far_send,
    far_recv,
    shard,
    rows_out,
    bias_sum,
    stats_dp,
    stats_t,
    local_sem,
    out_sem,
    wz_send,
    wz_recv,
    wf_send,
    wy_send,
    wy_recv,
    ax_send,
    ax_recv,
    as_send,
    as_recv,
    af_send,
    af_recv,
    rs_send,
    rs_recv,
    rx_send,
    rx_recv,
    gy_send,
    gy_recv,
    gz_send,
    gz_recv,
    sd_send,
    sd_recv,
    st_send,
    st_recv,
):
    d = lax.axis_index("dp")
    t = lax.axis_index("tensor")
    major, minor = lax.div(d, 2), lax.rem(d, 2)
    near = (2 * major + 1 - minor, t)
    pair, side = lax.div(t, 2), lax.rem(t, 2)
    sibling = (d, 2 * pair + 1 - side)
    middle = jnp.logical_and(major > 0, major < sz.major - 1)

    def far_slot(k):
        return 2 * flip_bits(major, k) + minor

    def near_slot(k):
        return 2 * flip_bits(major, k) + 1 - minor

    def far(k):
        return (far_slot(k), t)

    def cross_rank(k):
        return 2 * lax.rem(pair + k, sz.pairs) + side

    def cross_from(k):
        return 2 * lax.rem(pair + sz.pairs - k, sz.pairs) + side

    def remote(src, dst, send, recv, device):
        return pltpu.make_async_remote_copy(
            src_ref=src, dst_ref=dst, send_sem=send, recv_sem=recv, device_id=device, device_id_type=MESH
        )

    def same(block, send, recv, device):
        return remote(block, block, send, recv, device)

    far_steps = range(1, sz.major)
    cross_steps = range(1, sz.pairs)
    all_pieces = range(sz.pieces)

    def rows_of(p):
        return pl.ds(pl.multiple_of(p * sz.piece, 16), sz.piece)

    load_w = [pltpu.make_async_copy(weights_ref.at[l], w_in.at[l], local_sem.at[l]) for l in (0, 1)]
    load_frames = pltpu.make_async_copy(frames_ref, stage.at[0], local_sem.at[2])
    load_cot = pltpu.make_async_copy(cot_ref, stage.at[1], local_sem.at[3])
    load_biases = pltpu.make_async_copy(biases_ref, biases, local_sem.at[4])
    load_mask = pltpu.make_async_copy(mask_ref, mask, local_sem.at[5])
    for copy in (load_w[0], load_frames, load_w[1], load_cot, load_biases, load_mask):
        copy.start()

    barrier = pltpu.get_barrier_semaphore()
    for k in range(1, sz.dp):
        pl.semaphore_signal(barrier, inc=1, device_id=(lax.rem(d + k, sz.dp), t), device_id_type=MESH)
    for k in range(1, sz.tensor):
        pl.semaphore_signal(barrier, inc=1, device_id=(d, lax.rem(t + k, sz.tensor)), device_id_type=MESH)

    def weight_sends(l):
        block = w_all.at[l, d]
        direct = {k: same(block, wz_send.at[l, k], wz_recv.at[l, k], far(k)) for k in sz.far_order}
        return direct, same(block, wy_send.at[l, 0], wy_recv.at[l, 0], near)

    def weight_relay(l):
        return same(w_all.at[l, far_slot(2)], wf_send.at[l], wz_recv.at[l, 3], far(1))

    def weight_forward(l, k):
        return same(w_all.at[l, far_slot(k)], wy_send.at[l, k], wy_recv.at[l, k], near)

    def send_weights(l):
        direct, over = weight_sends(l)
        over.start()
        for k, copy in direct.items():
            if sz.relay and k == 3:
                pl.when(middle)(copy.start)
            else:
                copy.start()

    def weights_sent(l):
        direct, over = weight_sends(l)
        over.wait_send()
        for k, copy in direct.items():
            weight_forward(l, k).wait_send()
            if sz.relay and k == 3:

                @pl.when(middle)
                def _():
                    copy.wait_send()
                    weight_relay(l).wait_send()

            else:
                copy.wait_send()

    def forward_weights(l, k):
        same(w_all.at[l, far_slot(k)], wz_send.at[l, k], wz_recv.at[l, k], far(k)).wait_recv()
        if sz.relay and k == 2:
            pl.when(middle)(weight_relay(l).start)
        weight_forward(l, k).start()

    def weights_here(l):
        for k in range(sz.major):
            same(w_all.at[l, near_slot(k)], wy_send.at[l, k], wy_recv.at[l, k], near).wait_recv()

    def round_weights(l):
        load_w[l].wait()
        for tap in range(TAPS):
            w_all[l, d, :, tap * sz.out : (tap + 1) * sz.out] = w_in[
                l, pl.ds(tap, sz.own_in, stride=TAPS), :
            ].astype(sz.wire)

    def gather_sends(g, maps, p, rows):
        own = maps.at[t, rows]
        out = [same(own, ax_send.at[g, p, k], ax_recv.at[g, p, k], (d, cross_rank(k))) for k in cross_steps]
        out.append(same(own, as_send.at[g, p], as_recv.at[g, p], sibling))
        return out

    def gather_forward(g, maps, p, rows, k):
        return same(maps.at[cross_from(k), rows], af_send.at[g, p, k], af_recv.at[g, p, k], sibling)

    def gather_pass_on(g, maps, p, rows):
        for k in cross_steps:
            same(maps.at[cross_from(k), rows], ax_send.at[g, p, k], ax_recv.at[g, p, k], sibling).wait_recv()
            gather_forward(g, maps, p, rows, k).start()

    def gather_here(g, maps, p, rows):
        same(maps.at[sibling[1], rows], as_send.at[g, p], as_recv.at[g, p], sibling).wait_recv()
        for k in cross_steps:
            rank = 2 * lax.rem(pair + sz.pairs - k, sz.pairs) + 1 - side
            same(maps.at[rank, rows], af_send.at[g, p, k], af_recv.at[g, p, k], sibling).wait_recv()

    def gather_sent(g, maps, p, rows):
        for copy in gather_sends(g, maps, p, rows):
            copy.wait_send()
        for k in cross_steps:
            gather_forward(g, maps, p, rows, k).wait_send()

    whole = pl.ds(0, sz.span)

    def product(l, maps, group):
        rows = slice(group[0] * sz.piece, group[1] * sz.piece)
        left = jnp.concatenate([maps[q, rows] for q in range(sz.tensor)], axis=1)
        for start in range(0, sz.cols, WIDE):
            stop = min(start + WIDE, sz.cols)
            right = w_all[l, :, :, start:stop].reshape(sz.chan, stop - start).astype(BF16)
            spread[sz.halo + rows.start : sz.halo + rows.stop, start:stop] = jnp.dot(
                left, right, preferred_element_type=F32
            )

    def own_bias(l):
        return biases[l : l + 1, pl.ds(pl.multiple_of(t * sz.out, sz.out), sz.out)]

    def shifted_sum(p):
        sums = []
        for b in range(3):
            total = None
            for a in range(3):
                shift = sz.items * (sz.width * (a - 1) + b - 1)
                tap = 3 * a + b
                rows = pl.ds(pl.multiple_of(p * sz.piece + sz.halo + shift, 8), sz.piece)
                term = spread[rows, tap * sz.out : (tap + 1) * sz.out]
                total = term if total is None else total + term
            sums.append(total)
        return sums[1] + sums[0] * edges[0, rows_of(p)] + sums[2] * edges[1, rows_of(p)]

    def note_delta(l, p, delta):
        bias_sum[l] += jnp.sum(delta.reshape(sz.piece // 8, 8, sz.out), axis=0)
        rows = pl.ds(pl.multiple_of(p * sz.piece + sz.halo, 8), sz.piece)
        shifted[0, rows] = delta * edges[0, rows_of(p)]
        shifted[1, rows] = delta
        shifted[2, rows] = delta * edges[1, rows_of(p)]

    def spread_delta():
        @pl.loop(0, sz.pieces)
        def _(p):
            for a in range(3):
                for b in range(3):
                    shift = sz.items * (sz.width * (a - 1) + b - 1)
                    tap = 3 * a + b
                    rows = pl.ds(pl.multiple_of(p * sz.piece + sz.halo - shift, 8), sz.piece)
                    deltas[rows_of(p), tap * sz.out : (tap + 1) * sz.out] = shifted[b, rows].astype(BF16)

    def finish_four(first, last):
        @pl.loop(first, last)
        def _(p):
            act, slope = gelu_parts(shifted_sum(p) + own_bias(0))
            acts[t, rows_of(p)] = (act * edges[2, rows_of(p)]).astype(BF16)
            slope4[rows_of(p)] = slope * edges[2, rows_of(p)]
            for copy in gather_sends(1, acts, p, rows_of(p)):
                copy.start()

    def by_item(value):
        return (value.reshape(sz.piece // sz.items, sz.items, sz.out) * keep[...]).reshape(sz.piece, sz.out)

    def finish_five(first, last):
        @pl.loop(first, last)
        def _(p):
            act, slope = gelu_parts(shifted_sum(p) + own_bias(1))
            act5[rows_of(p)] = by_item(act).astype(BF16)
            delta = (by_item(cot[rows_of(p)].astype(F32)) * slope).astype(BF16).astype(F32)
            note_delta(1, p, delta)

    def part_copy(l, p):
        rows = rows_of(p)
        return remote(
            part_send.at[l, :, rows], part_recv.at[l, :, rows], rs_send.at[l, p], rs_recv.at[l, p], sibling
        )

    def cross_copy(l, p, k):
        rows = rows_of(p)
        return remote(
            cross_send.at[l, k, rows],
            cross_recv.at[l, k, rows],
            rx_send.at[l, p, k],
            rx_recv.at[l, p, k],
            (d, cross_rank(k)),
        )

    def back_product(l, group, which):
        blocks = [
            w_all[l, pl.ds((2 * j + which) * sz.slots, sz.slots)].reshape(sz.out, sz.cols) for j in range(sz.pairs)
        ]
        right = jnp.concatenate(blocks, axis=0).astype(BF16)
        left = deltas[group[0] * sz.piece : group[1] * sz.piece]
        out = lax.dot_general(left, right, (((1,), (1,)), ((), ())), preferred_element_type=F32)
        return [out[:, j * sz.out : (j + 1) * sz.out] for j in range(sz.pairs)]

    def back_to_sibling(l, group):
        rows = slice(group[0] * sz.piece, group[1] * sz.piece)
        for j, block in enumerate(back_product(l, group, 1 - side)):
            part_send[l, j, rows] = block.astype(BF16)
        for p in range(*group):
            part_copy(l, p).start()

    def back_own(l, group):
        rows = slice(group[0] * sz.piece, group[1] * sz.piece)
        for j, block in enumerate(back_product(l, group, side)):
            part_own[j, rows] = block

    def back_across(l, group):
        @pl.loop(*group)
        def _(p):
            part_copy(l, p).wait_recv()
            for k in cross_steps:
                j = lax.rem(pair + k, sz.pairs)
                total = part_own[j, rows_of(p)] + part_recv[l, j, rows_of(p)].astype(F32)
                cross_send[l, k, rows_of(p)] = total.astype(BF16)
                cross_copy(l, p, k).start()

    def back_products(l):
        one, two = sz.groups
        back_to_sibling(l, one)
        back_own(l, one)
        back_to_sibling(l, two)
        back_across(l, one)
        back_own(l, two)
        back_across(l, two)

    def back_total(l, p):
        total = part_own[pair, rows_of(p)] + part_recv[l, pair, rows_of(p)].astype(F32)
        for k in cross_steps:
            cross_copy(l, p, k).wait_recv()
            total += cross_recv[l, k, rows_of(p)].astype(F32)
        return total

    def near_copy(l, k):
        return remote(near_send.at[l, k], near_recv.at[l, k], gy_send.at[l, k], gy_recv.at[l, k], near)

    def far_copy(l, k):
        return remote(far_send.at[l, k], far_recv.at[l, k], gz_send.at[l, k], gz_recv.at[l, k], far(k))

    half = sz.tensor // 2
    far_half = [k for k in far_steps if k >= sz.major // 2]
    near_half = [k for k in far_steps if k < sz.major // 2]

    def grads_half(l, maps, other):
        own = lax.div(major, sz.major // 2)
        first = (1 - own if other else own) * half
        left = jnp.concatenate([maps[first + q] for q in range(half)], axis=1)
        into = pl.ds(first * sz.slots, half * sz.slots)
        for start in range(0, sz.cols, WIDE):
            stop = min(start + WIDE, sz.cols)
            product = lax.dot_general(left, deltas[:, start:stop], (((0,), (0,)), ((), ())), preferred_element_type=F32)
            kgrad[l, into, :, start:stop] = product.reshape(half * sz.slots, sz.own_in, stop - start)
        for k in far_half if other else [*near_half, 0]:
            near_send[l, k] = kgrad[l, near_slot(k)].astype(sz.wire)
            near_copy(l, k).start()

    def grads_far(l, k):
        near_copy(l, k).wait_recv()
        far_send[l, k] = (kgrad[l, far_slot(k)] + near_recv[l, k].astype(F32)).astype(sz.wire)
        far_copy(l, k).start()

    def grads_done(l):
        near_copy(l, 0).wait_recv()
        for k in far_steps:
            far_copy(l, k).wait_recv()
        total = kgrad[l, d] + near_recv[l, 0].astype(F32)
        for k in far_steps:
            total += far_recv[l, k].astype(F32)
        shard[...] = total
        squares = jnp.sum((total * total).reshape(sz.own_in // 8, 8, sz.cols), axis=0)
        for tap in range(TAPS):
            rows_out[l, pl.ds(tap, sz.own_in, stride=TAPS), :] = shard[:, tap * sz.out : (tap + 1) * sz.out]
        return sum(squares[:, tap * sz.out : (tap + 1) * sz.out] for tap in range(TAPS))

    rest = sz.halo + sz.span
    for first in (0, rest):
        spread[first : first + sz.halo, :] = jnp.zeros((sz.halo, sz.cols), F32)
        shifted[:, first : first + sz.halo, :] = jnp.zeros((3, sz.halo, sz.out), F32)

    @pl.loop(0, sz.pieces)
    def _(p):
        spot = lax.div(p * sz.piece + lax.broadcasted_iota(jnp.int32, (sz.piece, sz.out), 0), sz.items)
        column = lax.rem(spot, sz.width)
        edges[0, rows_of(p)] = (column > 0).astype(F32)
        edges[1, rows_of(p)] = (column < sz.width - 1).astype(F32)
        edges[2, rows_of(p)] = (spot < sz.spots).astype(F32)

    bias_sum[...] = jnp.zeros_like(bias_sum)
    tail = sz.span - 16
    cot[tail:] = jnp.zeros((16, sz.out), BF16)
    frames[t, tail:] = jnp.zeros((16, sz.out), BF16)

    round_weights(0)
    pl.semaphore_wait(barrier, sz.dp + sz.tensor - 2)
    send_weights(0)
    load_frames.wait()
    frames[t, 0 : sz.real] = stage[0]
    for copy in gather_sends(0, frames, 0, whole):
        copy.start()
    round_weights(1)
    send_weights(1)

    load_cot.wait()
    cot[0 : sz.real] = stage[1]
    load_biases.wait()
    load_mask.wait()
    item = lax.broadcasted_iota(jnp.int32, (sz.items, sz.out), 0)
    kept = jnp.zeros((sz.items, sz.out), F32)
    for n in range(sz.items):
        kept = jnp.where(item == n, mask[n].astype(F32), kept)
    keep[...] = kept

    gather_pass_on(0, frames, 0, whole)
    for k in far_steps:
        forward_weights(0, k)
    gather_here(0, frames, 0, whole)
    weights_here(0)

    one, two = sz.groups
    product(0, frames, one)
    finish_four(0, one[1] - 1)
    product(0, frames, two)
    finish_four(one[1] - 1, sz.pieces)

    for k in far_steps:
        forward_weights(1, k)
    stage[0] = acts[t, 0 : sz.real]
    save_act4 = pltpu.make_async_copy(stage.at[0], act4_out, out_sem.at[0])
    save_act4.start()

    for p in all_pieces:
        gather_pass_on(1, acts, p, rows_of(p))
    for p in all_pieces:
        gather_here(1, acts, p, rows_of(p))
    weights_here(1)
    product(1, acts, one)
    finish_five(0, one[1] - 1)
    product(1, acts, two)
    finish_five(one[1] - 1, sz.pieces)
    spread_delta()

    grads_half(1, acts, True)
    back_products(1)
    grads_half(1, acts, False)
    stage[1] = act5[0 : sz.real]
    save_act5 = pltpu.make_async_copy(stage.at[1], act5_out, out_sem.at[1])
    save_act5.start()
    for k in far_half:
        grads_far(1, k)

    @pl.loop(0, sz.pieces)
    def _(p):
        note_delta(0, p, (back_total(1, p) * slope4[rows_of(p)]).astype(BF16).astype(F32))

    spread_delta()
    grads_half(0, frames, True)
    for k in near_half:
        grads_far(1, k)
    grads_half(0, frames, False)
    back_products(0)
    for k in far_half:
        grads_far(0, k)
    squares = grads_done(1)
    save_grads = [pltpu.make_async_copy(rows_out.at[l], grads_out.at[l], out_sem.at[3 + l]) for l in (0, 1)]
    save_grads[1].start()
    for k in near_half:
        grads_far(0, k)

    @pl.loop(0, sz.pieces)
    def _(p):
        igrad[rows_of(p)] = back_total(0, p)

    save_igrad = pltpu.make_async_copy(igrad.at[0 : sz.real], igrad_out, out_sem.at[2])
    save_igrad.start()

    squares += grads_done(0)
    save_grads[0].start()

    stats_dp[d, 0:1, :] = jnp.sum(squares, axis=0, keepdims=True)
    for l in (0, 1):
        stats_dp[d, l + 1 : l + 2, :] = jnp.sum(bias_sum[l], axis=0, keepdims=True)
    stats_dp[d, 3:8, :] = jnp.zeros((5, sz.out), F32)

    def stats_over_dp(k, slot):
        return same(stats_dp.at[slot], sd_send.at[k], sd_recv.at[k], (lax.rem(d + k, sz.dp), t))

    def stats_over_tensor(k, slot):
        return same(stats_t.at[slot], st_send.at[k], st_recv.at[k], (d, lax.rem(t + k, sz.tensor)))

    for k in range(1, sz.dp):
        stats_over_dp(k, d).start()
    for k in range(1, sz.dp):
        stats_over_dp(k, lax.rem(d + sz.dp - k, sz.dp)).wait_recv()
    total = stats_dp[0]
    for slot in range(1, sz.dp):
        total += stats_dp[slot]
    stats_t[t] = total
    for k in range(1, sz.tensor):
        stats_over_tensor(k, t).start()
    for k in range(1, sz.tensor):
        stats_over_tensor(k, lax.rem(t + sz.tensor - k, sz.tensor)).wait_recv()
    save_stats = pltpu.make_async_copy(stats_t, stats_out, out_sem.at[5])
    save_stats.start()

    for l in (0, 1):
        weights_sent(l)
        for k in far_steps:
            far_copy(l, k).wait_send()
        for k in range(sz.major):
            near_copy(l, k).wait_send()

        @pl.loop(0, sz.pieces)
        def _(p):
            part_copy(l, p).wait_send()
            for k in cross_steps:
                cross_copy(l, p, k).wait_send()

    gather_sent(0, frames, 0, whole)

    @pl.loop(0, sz.pieces)
    def _(p):
        gather_sent(1, acts, p, rows_of(p))

    for k in range(1, sz.dp):
        stats_over_dp(k, d).wait_send()
    for k in range(1, sz.tensor):
        stats_over_tensor(k, t).wait_send()
    for copy in (save_act4, save_act5, save_igrad, *save_grads, save_stats):
        copy.wait()


def train_step(sz, frames, item_mask, weights, biases, cotangent):
    sem = pltpu.SemaphoreType.DMA
    vmem = pltpu.VMEM
    maps = (sz.span, sz.out)
    block = (sz.own_in, sz.cols)
    shapes = [
        vmem((2, sz.rows, sz.out), F32),
        vmem((2, sz.real, sz.out), BF16),
        vmem(maps, BF16),
        vmem((2, sz.chan), F32),
        pltpu.SMEM((sz.items,), jnp.int32),
        vmem((sz.items, sz.out), F32),
        vmem((2, sz.dp, *block), sz.wire),
        vmem((sz.tensor, *maps), BF16),
        vmem((sz.tensor, *maps), BF16),
        vmem((sz.span + 2 * sz.halo, sz.cols), F32),
        vmem((3, *maps), F32),
        vmem(maps, F32),
        vmem(maps, BF16),
        vmem((3, sz.span + 2 * sz.halo, sz.out), F32),
        vmem((sz.span, sz.cols), BF16),
        vmem((2, sz.pairs, *maps), BF16),
        vmem((2, sz.pairs, *maps), BF16),
        vmem((sz.pairs, *maps), F32),
        vmem((2, sz.pairs, *maps), BF16),
        vmem((2, sz.pairs, *maps), BF16),
        vmem(maps, F32),
        vmem((2, sz.dp, *block), F32),
        vmem((2, sz.major, *block), sz.wire),
        vmem((2, sz.major, *block), sz.wire),
        vmem((2, sz.major, *block), sz.wire),
        vmem((2, sz.major, *block), sz.wire),
        vmem(block, F32),
        vmem((2, sz.rows, sz.out), F32),
        vmem((2, 8, sz.out), F32),
        vmem((sz.dp, 8, sz.out), F32),
        vmem((sz.tensor, 8, sz.out), F32),
        sem((6,)),
        sem((6,)),
        sem((2, sz.major)),
        sem((2, sz.major)),
        sem((2,)),
        sem((2, sz.major)),
        sem((2, sz.major)),
        sem((2, sz.pieces, sz.pairs)),
        sem((2, sz.pieces, sz.pairs)),
        sem((2, sz.pieces)),
        sem((2, sz.pieces)),
        sem((2, sz.pieces, sz.pairs)),
        sem((2, sz.pieces, sz.pairs)),
        sem((2, sz.pieces)),
        sem((2, sz.pieces)),
        sem((2, sz.pieces, sz.pairs)),
        sem((2, sz.pieces, sz.pairs)),
        sem((2, sz.major)),
        sem((2, sz.major)),
        sem((2, sz.major)),
        sem((2, sz.major)),
        sem((sz.dp,)),
        sem((sz.dp,)),
        sem((sz.tensor,)),
        sem((sz.tensor,)),
    ]
    anywhere = pl.BlockSpec(memory_space=pl.ANY)
    macs = 6 * sz.real * TAPS * sz.chan * sz.out
    rows = (sz.real, sz.out)
    return pl.pallas_call(
        functools.partial(body, sz),
        out_shape=[
            jax.ShapeDtypeStruct(rows, BF16),
            jax.ShapeDtypeStruct(rows, BF16),
            jax.ShapeDtypeStruct(rows, F32),
            jax.ShapeDtypeStruct((2, sz.rows, sz.out), F32),
            jax.ShapeDtypeStruct((sz.tensor, 8, sz.out), F32),
        ],
        in_specs=[anywhere] * 5,
        out_specs=[anywhere] * 5,
        scratch_shapes=shapes,
        compiler_params=pltpu.CompilerParams(
            collective_id=0, has_side_effects=True, vmem_limit_bytes=60 * 1024 * 1024
        ),
        cost_estimate=pl.CostEstimate(flops=2 * macs, bytes_accessed=6_000_000, transcendentals=0),
        name="train_step",
    )(frames, item_mask, weights, biases, cotangent)


def finish_body(
    sz,
    act4_ref,
    act5_ref,
    igrad_ref,
    grads_ref,
    stats_ref,
    weights_ref,
    first_ref,
    second_ref,
    biases,
    bias_first,
    bias_second,
    act4_out,
    act5_out,
    igrad_out,
    norm_out,
    weights_out,
    first_out,
    second_out,
    biases_out,
    bias_first_out,
    bias_second_out,
    stats,
    maps,
    igrad,
    olds,
    news,
    in_sem,
    out_sem,
    move_sem,
):
    sources = (weights_ref, grads_ref, first_ref, second_ref)
    targets = (weights_out, first_out, second_out)
    loads = [
        [pltpu.make_async_copy(ref.at[l], olds.at[l, i], in_sem.at[l, i]) for i, ref in enumerate(sources)]
        for l in (0, 1)
    ]
    stores = [
        [pltpu.make_async_copy(news.at[l, i], ref.at[l], out_sem.at[l, i]) for i, ref in enumerate(targets)]
        for l in (0, 1)
    ]
    moves = (
        (act4_ref, maps.at[0], act4_out),
        (act5_ref, maps.at[1], act5_out),
        (igrad_ref, igrad, igrad_out),
    )
    moves_in = [pltpu.make_async_copy(src, held, move_sem.at[0, i]) for i, (src, held, _) in enumerate(moves)]
    moves_out = [pltpu.make_async_copy(held, dst, move_sem.at[1, i]) for i, (_, held, dst) in enumerate(moves)]
    load_stats = pltpu.make_async_copy(stats_ref, stats, move_sem.at[0, 3])
    for copy in (load_stats, *loads[0], *moves_in, *loads[1]):
        copy.start()
    load_stats.wait()
    bias_grad = jnp.concatenate([stats[q, 1:3, :] for q in range(sz.tensor)], axis=1)
    squares = jnp.sum(stats[:, 0, :], axis=(0, 1), keepdims=True) + jnp.sum(
        bias_grad * bias_grad, axis=(0, 1), keepdims=True
    )
    grad_norm = jnp.sqrt(squares)
    factor = jnp.minimum(1.0, CLIP_NORM / (grad_norm + 1e-06))
    norm_out[...] = grad_norm
    biases_out[...], bias_first_out[...], bias_second_out[...] = adam_update(
        biases[...], bias_grad * factor, bias_first[...], bias_second[...], BIAS_RATE, 0.0
    )
    for l in (0, 1):
        for copy in loads[l]:
            copy.wait()
        news[l, 0], news[l, 1], news[l, 2] = adam_update(
            olds[l, 0], olds[l, 1] * factor, olds[l, 2], olds[l, 3], RATE, DECAY
        )
        for copy in stores[l]:
            copy.start()
        if l == 0:
            for here, there in zip(moves_in, moves_out):
                here.wait()
                there.start()
    for copy in (*stores[0], *stores[1], *moves_out):
        copy.wait()


def finish(sz, act4, act5, igrad, grads, stats, weights, first, second, biases, bias_first, bias_second):
    anywhere = pl.BlockSpec(memory_space=pl.ANY)
    inside = pl.BlockSpec(memory_space=pltpu.VMEM)
    outside = pl.BlockSpec(memory_space=pltpu.HBM)
    like = lambda x: jax.ShapeDtypeStruct(x.shape, x.dtype)
    sem = pltpu.SemaphoreType.DMA
    return pl.pallas_call(
        functools.partial(finish_body, sz),
        out_shape=[
            like(act4),
            like(act5),
            like(igrad),
            jax.ShapeDtypeStruct((1, 1), F32),
            like(weights),
            like(first),
            like(second),
            like(biases),
            like(bias_first),
            like(bias_second),
        ],
        in_specs=[outside] * 5 + [anywhere] * 3 + [inside] * 3,
        out_specs=[outside] * 3 + [inside] + [outside] * 3 + [inside] * 3,
        scratch_shapes=[
            pltpu.VMEM((sz.tensor, 8, sz.out), F32),
            pltpu.VMEM((2, sz.real, sz.out), BF16),
            pltpu.VMEM((sz.real, sz.out), F32),
            pltpu.VMEM((2, 4, sz.rows, sz.out), F32),
            pltpu.VMEM((2, 3, sz.rows, sz.out), F32),
            sem((2, 4)),
            sem((2, 3)),
            sem((2, 4)),
        ],
        compiler_params=pltpu.CompilerParams(vmem_limit_bytes=60 * 1024 * 1024),
        cost_estimate=pl.CostEstimate(flops=5_000_000, bytes_accessed=7_000_000, transcendentals=0),
        name="clip_and_adamw",
    )(act4, act5, igrad, grads, stats, weights, first, second, biases, bias_first, bias_second)


def on_device(
    mesh,
    frames,
    item_mask,
    weights,
    biases,
    cotangent,
    weight_first,
    weight_second,
    bias_first,
    bias_second,
):
    sz = Sizes(mesh, frames.shape, weights.shape)

    def flat(maps):
        return jnp.transpose(maps, (1, 2, 0, 3)).reshape(sz.real, sz.out)

    def square(rows):
        return jnp.transpose(rows.reshape(sz.height, sz.width, sz.items, sz.out), (2, 0, 1, 3))

    made = train_step(sz, flat(frames), item_mask, weights, biases, flat(cotangent))
    act_four, act_five, input_grad, grad_norm, *rest = finish(
        sz, *made, weights, weight_first, weight_second, biases, bias_first, bias_second
    )
    return (square(act_four), square(act_five), square(input_grad), grad_norm.reshape(()), *rest)


def solution(mesh):
    split = P("dp", None, None, "tensor")
    rows = P(None, "dp", "tensor")
    in_specs = (split, P("dp"), rows, P(), split, rows, rows, P(), P())
    out_specs = (split, split, split, P(), rows, rows, rows, P(), P(), P())
    return jax.shard_map(
        functools.partial(on_device, mesh), mesh=mesh, in_specs=in_specs, out_specs=out_specs, check_vma=False
    )
```

time: 116 us -> 91.6 us (0.79)
  Pallas kernels: 98.8 us -> 90.8 us
  local copies, waits for them, and re-layouts: 7.16 us -> 0 us
  other arithmetic: 6.59 us -> 0 us
  between operations: 3.23 us -> 0.65 us
    pallas_call x1, Pallas kernels: 98.8 us -> 86 us  [train_step(): pl.pallas_call(functools.partial(body, sz), out_shape=[jax.ShapeDtypeStru...]
    pallas_call x0 -> x1, Pallas kernels: none -> 4.73 us  [finish(): pl.pallas_call(functools.partial(finish_body, sz), out_shape=[like(act4),...]
    sub x2 -> x0, other arithmetic: 3.94 us -> none  [adam_update(): param - rate * (corrected / scaled + decay * param)]
    slice x3 -> x0, local copies, waits for them, and re-layouts: 3.77 us -> none  [square(): return rows[:, :sz.spots].reshape(sz.items, sz.height, sz.width, sz.out)]
    reduce_sum x2 -> x0, other arithmetic: 2.65 us -> none  [the longest x1 1.33 us: on_device(): jnp.sum(bias_grad * bias_grad)]
    pad x2 -> x0, local copies, waits for them, and re-layouts: 1.53 us -> none  [flat(): return jnp.pad(rows, ((0, 0), (0, sz.span - sz.spots), (0, 0)))]
where the time goes in v2:
time: 91.6 us; the launch traced here: 91.4 us
  Pallas kernels  90.8 us (99%)
    pallas_call x1, Pallas kernels, train_step(): pl.pallas_call(functools.partial(body, sz), out_shape=[jax.ShapeDtypeStru...  86 us
    pallas_call x1, Pallas kernels, finish(): pl.pallas_call(functools.partial(finish_body, sz), out_shape=[like(act4),...  4.73 us

profile of v2, /device:TPU:0, one launch (start us, length us, event | category | flops | bytes accessed | tf_op | source)
XLA Modules:
  0.0 91.4 jit_solution(3710233276008377993)
XLA Ops:
  0.6 86.0 %train_step.1 = (bf16[1352,128]{1,0:T(8,128)(2,1)}, bf16[1352,128]{1,0:T(8,128)(2,1)}, f32[1352,128]{1,0:T(8,128)}, f32[2,576,128]{2,1,0:T(8,128)}, f32[4,8,128]{2,1,0:T(8,128)}) custom-call(bf16[1352,128]{1,0:T(8,128)(2,1)} %bitcast.17, s32[8]{0:T(128)} %mask_ref.1, f32[2,576,128]{2,1,0:T(8,128)} %weights_ref.3, f32[2,512]{1,0:T(2,128)} %biases.1, ...), custom_call_target="tpu_custom_call" | custom-call | flops 9569304576 | bytes 6000000 | tf_op jit(solution)/shard_map/train_step/pallas_call | solution.py:669
  86.7 4.7 %clip_and_adamw.1 = (bf16[1352,128]{1,0:T(8,128)(2,1)}, bf16[1352,128]{1,0:T(8,128)(2,1)}, f32[1352,128]{1,0:T(8,128)}, f32[1,1]{1,0:T(1,128)}, f32[2,576,128]{2...) custom-call(bf16[1352,128]{1,0:T(8,128)(2,1)} %get-tuple-element.25., ...), custom_call_target="tpu_custom_call" | custom-call | flops 5000000 | bytes 7000000 | tf_op jit(solution)/shard_map/clip_and_adamw/pallas_call | solution.py:774

commit v3 on v2

--- a/solution.py
+++ b/solution.py
@@ -46,8 +46,8 @@
 def adam_update(param, grad, first, second, rate, decay):
     first_new = BETA_ONE * first + (1.0 - BETA_ONE) * grad
     second_new = BETA_TWO * second + (1.0 - BETA_TWO) * grad * grad
-    corrected = first_new / (1.0 - BETA_ONE**STEP)
-    scaled = jnp.sqrt(second_new / (1.0 - BETA_TWO**STEP)) + EPSILON
+    corrected = first_new * (1.0 / (1.0 - BETA_ONE**STEP))
+    scaled = jnp.sqrt(second_new * (1.0 / (1.0 - BETA_TWO**STEP))) + EPSILON
     return (param - rate * (corrected / scaled + decay * param), first_new, second_new)
 
 
@@ -71,8 +71,9 @@
         self.piece = self.span // self.pieces
         self.groups = ((0, self.pieces // 2), (self.pieces // 2, self.pieces))
         self.wire = BF16 if self.own_in % 16 == 0 else F32
-        self.relay = self.major == 4
-        self.far_order = (2, 1, 3) if self.relay else tuple(range(1, self.major))
+        cut = (TAPS + 1) // 2 * self.out
+        self.parts = ((0, cut), (cut, self.cols))
+        self.devices = self.dp * self.tensor
 
 
 def body(
@@ -116,13 +117,13 @@
     shard,
     rows_out,
     bias_sum,
-    stats_dp,
+    stats_all,
     stats_t,
     local_sem,
     out_sem,
-    wz_send,
+    wu_send,
+    wd_send,
     wz_recv,
-    wf_send,
     wy_send,
     wy_recv,
     ax_send,
@@ -139,8 +140,6 @@
     gy_recv,
     gz_send,
     gz_recv,
-    sd_send,
-    sd_recv,
     st_send,
     st_recv,
 ):
@@ -150,7 +149,6 @@
     near = (2 * major + 1 - minor, t)
     pair, side = lax.div(t, 2), lax.rem(t, 2)
     sibling = (d, 2 * pair + 1 - side)
-    middle = jnp.logical_and(major > 0, major < sz.major - 1)
 
     def far_slot(k):
         return 2 * flip_bits(major, k) + minor
@@ -175,12 +173,27 @@
     def same(block, send, recv, device):
         return remote(block, block, send, recv, device)
 
+    all_pieces = range(sz.pieces)
+
+    def rows_of(p):
+        return pl.ds(pl.multiple_of(p * sz.piece, 16), sz.piece)
+
     far_steps = range(1, sz.major)
     cross_steps = range(1, sz.pairs)
-    all_pieces = range(sz.pieces)
-
-    def rows_of(p):
-        return pl.ds(pl.multiple_of(p * sz.piece, 16), sz.piece)
+    above, below = major + 1 < sz.major, major > 0
+    up, down = (2 * (major + 1) + minor, t), (2 * (major - 1) + minor, t)
+
+    barrier = pltpu.get_barrier_semaphore()
+
+    def greet(device):
+        pl.semaphore_signal(barrier, inc=1, device_id=device, device_id_type=MESH)
+
+    pl.when(above)(lambda: greet(up))
+    pl.when(below)(lambda: greet(down))
+    greet(near)
+    for k in cross_steps:
+        greet((d, cross_rank(k)))
+    greet(sibling)
 
     load_w = [pltpu.make_async_copy(weights_ref.at[l], w_in.at[l], local_sem.at[l]) for l in (0, 1)]
     load_frames = pltpu.make_async_copy(frames_ref, stage.at[0], local_sem.at[2])
@@ -190,56 +203,68 @@
     for copy in (load_w[0], load_frames, load_w[1], load_cot, load_biases, load_mask):
         copy.start()
 
-    barrier = pltpu.get_barrier_semaphore()
-    for k in range(1, sz.dp):
-        pl.semaphore_signal(barrier, inc=1, device_id=(lax.rem(d + k, sz.dp), t), device_id_type=MESH)
-    for k in range(1, sz.tensor):
-        pl.semaphore_signal(barrier, inc=1, device_id=(d, lax.rem(t + k, sz.tensor)), device_id_type=MESH)
-
-    def weight_sends(l):
-        block = w_all.at[l, d]
-        direct = {k: same(block, wz_send.at[l, k], wz_recv.at[l, k], far(k)) for k in sz.far_order}
-        return direct, same(block, wy_send.at[l, 0], wy_recv.at[l, 0], near)
-
-    def weight_relay(l):
-        return same(w_all.at[l, far_slot(2)], wf_send.at[l], wz_recv.at[l, 3], far(1))
-
-    def weight_forward(l, k):
-        return same(w_all.at[l, far_slot(k)], wy_send.at[l, k], wy_recv.at[l, k], near)
-
-    def send_weights(l):
-        direct, over = weight_sends(l)
-        over.start()
-        for k, copy in direct.items():
-            if sz.relay and k == 3:
-                pl.when(middle)(copy.start)
-            else:
-                copy.start()
-
-    def weights_sent(l):
-        direct, over = weight_sends(l)
-        over.wait_send()
-        for k, copy in direct.items():
-            weight_forward(l, k).wait_send()
-            if sz.relay and k == 3:
-
-                @pl.when(middle)
-                def _():
-                    copy.wait_send()
-                    weight_relay(l).wait_send()
-
-            else:
-                copy.wait_send()
-
-    def forward_weights(l, k):
-        same(w_all.at[l, far_slot(k)], wz_send.at[l, k], wz_recv.at[l, k], far(k)).wait_recv()
-        if sz.relay and k == 2:
-            pl.when(middle)(weight_relay(l).start)
-        weight_forward(l, k).start()
-
-    def weights_here(l):
-        for k in range(sz.major):
-            same(w_all.at[l, near_slot(k)], wy_send.at[l, k], wy_recv.at[l, k], near).wait_recv()
+    def weight_block(l, part, slot):
+        first, last = sz.parts[part]
+        return w_all.at[l, slot, :, first:last]
+
+    def weight_up(l, part, source):
+        return same(
+            weight_block(l, part, 2 * source + minor), wu_send.at[l, part, source], wz_recv.at[l, part, source], up
+        )
+
+    def weight_down(l, part, source):
+        return same(
+            weight_block(l, part, 2 * source + minor), wd_send.at[l, part, source], wz_recv.at[l, part, source], down
+        )
+
+    def weight_over(l, part, source):
+        return same(
+            weight_block(l, part, 2 * source + minor), wy_send.at[l, part, source], wy_recv.at[l, part, source], near
+        )
+
+    def weights_out(l, part):
+        pl.when(above)(weight_up(l, part, major).start)
+        pl.when(below)(weight_down(l, part, major).start)
+
+    def weights_on(l, part):
+        @pl.loop(1, sz.major)
+        def _(step):
+            @pl.when(major - step >= 0)
+            def _():
+                source = major - step
+                weight_up(l, part, source).wait_recv()
+                pl.when(above)(weight_up(l, part, source).start)
+                weight_over(l, part, source).start()
+
+            @pl.when(major + step < sz.major)
+            def _():
+                source = major + step
+                weight_down(l, part, source).wait_recv()
+                pl.when(below)(weight_down(l, part, source).start)
+                weight_over(l, part, source).start()
+
+    def weights_here(l, part):
+        @pl.loop(0, sz.major)
+        def _(source):
+            same(
+                weight_block(l, part, 2 * source + 1 - minor),
+                wy_send.at[l, part, source],
+                wy_recv.at[l, part, source],
+                near,
+            ).wait_recv()
+
+    def weights_sent(l, part):
+        @pl.loop(0, sz.major)
+        def _(source):
+            weight_over(l, part, source).wait_send()
+
+            @pl.when(jnp.logical_and(source <= major, above))
+            def _():
+                weight_up(l, part, source).wait_send()
+
+            @pl.when(jnp.logical_and(source >= major, below))
+            def _():
+                weight_down(l, part, source).wait_send()
 
     def round_weights(l):
         load_w[l].wait()
@@ -276,11 +301,12 @@
 
     whole = pl.ds(0, sz.span)
 
-    def product(l, maps, group):
+    def product(l, part, maps, group):
         rows = slice(group[0] * sz.piece, group[1] * sz.piece)
         left = jnp.concatenate([maps[q, rows] for q in range(sz.tensor)], axis=1)
-        for start in range(0, sz.cols, WIDE):
-            stop = min(start + WIDE, sz.cols)
+        first, last = sz.parts[part]
+        for start in range(first, last, WIDE):
+            stop = min(start + WIDE, last)
             right = w_all[l, :, :, start:stop].reshape(sz.chan, stop - start).astype(BF16)
             spread[sz.halo + rows.start : sz.halo + rows.stop, start:stop] = jnp.dot(
                 left, right, preferred_element_type=F32
@@ -443,34 +469,36 @@
             rows_out[l, pl.ds(tap, sz.own_in, stride=TAPS), :] = shard[:, tap * sz.out : (tap + 1) * sz.out]
         return sum(squares[:, tap * sz.out : (tap + 1) * sz.out] for tap in range(TAPS))
 
-    rest = sz.halo + sz.span
-    for first in (0, rest):
-        spread[first : first + sz.halo, :] = jnp.zeros((sz.halo, sz.cols), F32)
-        shifted[:, first : first + sz.halo, :] = jnp.zeros((3, sz.halo, sz.out), F32)
-
-    @pl.loop(0, sz.pieces)
-    def _(p):
-        spot = lax.div(p * sz.piece + lax.broadcasted_iota(jnp.int32, (sz.piece, sz.out), 0), sz.items)
-        column = lax.rem(spot, sz.width)
-        edges[0, rows_of(p)] = (column > 0).astype(F32)
-        edges[1, rows_of(p)] = (column < sz.width - 1).astype(F32)
-        edges[2, rows_of(p)] = (spot < sz.spots).astype(F32)
-
-    bias_sum[...] = jnp.zeros_like(bias_sum)
+    round_weights(0)
+    joined = 1 + sz.pairs + above.astype(jnp.int32) + below.astype(jnp.int32)
+    pl.semaphore_wait(barrier, joined)
+    for part in (0, 1):
+        weight_over(0, part, major).start()
+        weights_out(0, part)
     tail = sz.span - 16
-    cot[tail:] = jnp.zeros((16, sz.out), BF16)
     frames[t, tail:] = jnp.zeros((16, sz.out), BF16)
-
-    round_weights(0)
-    pl.semaphore_wait(barrier, sz.dp + sz.tensor - 2)
-    send_weights(0)
     load_frames.wait()
     frames[t, 0 : sz.real] = stage[0]
     for copy in gather_sends(0, frames, 0, whole):
         copy.start()
     round_weights(1)
-    send_weights(1)
-
+    for part in (0, 1):
+        weight_over(1, part, major).start()
+
+    rest = sz.halo + sz.span
+    for first in (0, rest):
+        spread[first : first + sz.halo, :] = jnp.zeros((sz.halo, sz.cols), F32)
+        shifted[:, first : first + sz.halo, :] = jnp.zeros((3, sz.halo, sz.out), F32)
+    edges[...] = jnp.ones_like(edges)
+    nothing = jnp.zeros((sz.items, sz.out), F32)
+    for i in range(sz.height):
+        for e, j in ((0, 0), (1, sz.width - 1)):
+            first = (i * sz.width + j) * sz.items
+            edges[e, first : first + sz.items, :] = nothing
+    edges[2, sz.real :, :] = jnp.zeros((sz.span - sz.real, sz.out), F32)
+    bias_sum[...] = jnp.zeros_like(bias_sum)
+
+    cot[tail:] = jnp.zeros((16, sz.out), BF16)
     load_cot.wait()
     cot[0 : sz.real] = stage[1]
     load_biases.wait()
@@ -481,32 +509,40 @@
         kept = jnp.where(item == n, mask[n].astype(F32), kept)
     keep[...] = kept
 
+    one, two = sz.groups
+    weights_on(0, 0)
+    for part in (0, 1):
+        weights_out(1, part)
     gather_pass_on(0, frames, 0, whole)
-    for k in far_steps:
-        forward_weights(0, k)
+    weights_on(0, 1)
     gather_here(0, frames, 0, whole)
-    weights_here(0)
-
-    one, two = sz.groups
-    product(0, frames, one)
+    weights_here(0, 0)
+    product(0, 0, frames, one)
+    product(0, 0, frames, two)
+    weights_here(0, 1)
+    product(0, 1, frames, one)
     finish_four(0, one[1] - 1)
-    product(0, frames, two)
+    product(0, 1, frames, two)
     finish_four(one[1] - 1, sz.pieces)
 
-    for k in far_steps:
-        forward_weights(1, k)
+    weights_on(1, 0)
     stage[0] = acts[t, 0 : sz.real]
     save_act4 = pltpu.make_async_copy(stage.at[0], act4_out, out_sem.at[0])
     save_act4.start()
-
-    for p in all_pieces:
+    for p in range(*one):
+        gather_pass_on(1, acts, p, rows_of(p))
+    weights_on(1, 1)
+    for p in range(*two):
         gather_pass_on(1, acts, p, rows_of(p))
     for p in all_pieces:
         gather_here(1, acts, p, rows_of(p))
-    weights_here(1)
-    product(1, acts, one)
+    weights_here(1, 0)
+    product(1, 0, acts, one)
+    product(1, 0, acts, two)
+    weights_here(1, 1)
+    product(1, 1, acts, one)
     finish_five(0, one[1] - 1)
-    product(1, acts, two)
+    product(1, 1, acts, two)
     finish_five(one[1] - 1, sz.pieces)
     spread_delta()
 
@@ -547,34 +583,36 @@
     squares += grads_done(0)
     save_grads[0].start()
 
-    stats_dp[d, 0:1, :] = jnp.sum(squares, axis=0, keepdims=True)
+    me = d * sz.tensor + t
+    stats_all[me, 0:1, :] = jnp.sum(squares, axis=0, keepdims=True)
     for l in (0, 1):
-        stats_dp[d, l + 1 : l + 2, :] = jnp.sum(bias_sum[l], axis=0, keepdims=True)
-    stats_dp[d, 3:8, :] = jnp.zeros((5, sz.out), F32)
-
-    def stats_over_dp(k, slot):
-        return same(stats_dp.at[slot], sd_send.at[k], sd_recv.at[k], (lax.rem(d + k, sz.dp), t))
-
-    def stats_over_tensor(k, slot):
-        return same(stats_t.at[slot], st_send.at[k], st_recv.at[k], (d, lax.rem(t + k, sz.tensor)))
-
-    for k in range(1, sz.dp):
-        stats_over_dp(k, d).start()
-    for k in range(1, sz.dp):
-        stats_over_dp(k, lax.rem(d + sz.dp - k, sz.dp)).wait_recv()
-    total = stats_dp[0]
-    for slot in range(1, sz.dp):
-        total += stats_dp[slot]
-    stats_t[t] = total
-    for k in range(1, sz.tensor):
-        stats_over_tensor(k, t).start()
-    for k in range(1, sz.tensor):
-        stats_over_tensor(k, lax.rem(t + sz.tensor - k, sz.tensor)).wait_recv()
+        stats_all[me, l + 1 : l + 2, :] = jnp.sum(bias_sum[l], axis=0, keepdims=True)
+    stats_all[me, 3:8, :] = jnp.zeros((5, sz.out), F32)
+
+    def stats_copy(k, slot):
+        other = lax.rem(me + k, sz.devices)
+        device = (lax.div(other, sz.tensor), lax.rem(other, sz.tensor))
+        return same(stats_all.at[slot], st_send.at[k], st_recv.at[k], device)
+
+    @pl.loop(1, sz.devices)
+    def _(k):
+        stats_copy(k, me).start()
+
+    @pl.loop(1, sz.devices)
+    def _(k):
+        stats_copy(k, lax.rem(me + sz.devices - k, sz.devices)).wait_recv()
+
+    for q in range(sz.tensor):
+        total = stats_all[q]
+        for slot in range(q + sz.tensor, sz.devices, sz.tensor):
+            total += stats_all[slot]
+        stats_t[q] = total
     save_stats = pltpu.make_async_copy(stats_t, stats_out, out_sem.at[5])
     save_stats.start()
 
     for l in (0, 1):
-        weights_sent(l)
+        for part in (0, 1):
+            weights_sent(l, part)
         for k in far_steps:
             far_copy(l, k).wait_send()
         for k in range(sz.major):
@@ -592,10 +630,10 @@
     def _(p):
         gather_sent(1, acts, p, rows_of(p))
 
-    for k in range(1, sz.dp):
-        stats_over_dp(k, d).wait_send()
-    for k in range(1, sz.tensor):
-        stats_over_tensor(k, t).wait_send()
+    @pl.loop(1, sz.devices)
+    def _(k):
+        stats_copy(k, me).wait_send()
+
     for copy in (save_act4, save_act5, save_igrad, *save_grads, save_stats):
         copy.wait()
 
@@ -635,15 +673,15 @@
         vmem(block, F32),
         vmem((2, sz.rows, sz.out), F32),
         vmem((2, 8, sz.out), F32),
-        vmem((sz.dp, 8, sz.out), F32),
+        vmem((sz.devices, 8, sz.out), F32),
         vmem((sz.tensor, 8, sz.out), F32),
         sem((6,)),
         sem((6,)),
-        sem((2, sz.major)),
-        sem((2, sz.major)),
-        sem((2,)),
-        sem((2, sz.major)),
-        sem((2, sz.major)),
+        sem((2, 2, sz.major)),
+        sem((2, 2, sz.major)),
+        sem((2, 2, sz.major)),
+        sem((2, 2, sz.major)),
+        sem((2, 2, sz.major)),
         sem((2, sz.pieces, sz.pairs)),
         sem((2, sz.pieces, sz.pairs)),
         sem((2, sz.pieces)),
@@ -658,10 +696,8 @@
         sem((2, sz.major)),
         sem((2, sz.major)),
         sem((2, sz.major)),
-        sem((sz.dp,)),
-        sem((sz.dp,)),
-        sem((sz.tensor,)),
-        sem((sz.tensor,)),
+        sem((sz.devices,)),
+        sem((sz.devices,)),
     ]
     anywhere = pl.BlockSpec(memory_space=pl.ANY)
     macs = 6 * sz.real * TAPS * sz.chan * sz.out

time: 91.6 us -> 85.8 us (0.937)
  Pallas kernels: 90.8 us -> 85 us
    pallas_call x1, Pallas kernels: 86 us -> 80.2 us  [train_step(): pl.pallas_call(functools.partial(body, sz), out_shape=[jax.ShapeDtypeStru...]
where the time goes in v3:
time: 85.8 us; the launch traced here: 85.6 us
  Pallas kernels  85 us (99%)
    pallas_call x1, Pallas kernels, train_step(): pl.pallas_call(functools.partial(body, sz), out_shape=[jax.ShapeDtypeStru...  80.2 us
    pallas_call x1, Pallas kernels, finish(): pl.pallas_call(functools.partial(finish_body, sz), out_shape=[like(act4),...  4.73 us

profile of v3, /device:TPU:0, one launch (start us, length us, event | category | flops | bytes accessed | tf_op | source)
XLA Modules:
  0.0 85.6 jit_solution(6284117608655848214)
XLA Ops:
  0.6 80.2 %train_step.1 = (bf16[1352,128]{1,0:T(8,128)(2,1)}, bf16[1352,128]{1,0:T(8,128)(2,1)}, f32[1352,128]{1,0:T(8,128)}, f32[2,576,128]{2,1,0:T(8,128)}, f32[4,8,128]{2,1,0:T(8,128)}) custom-call(bf16[1352,128]{1,0:T(8,128)(2,1)} %bitcast.17, s32[8]{0:T(128)} %mask_ref.1, f32[2,576,128]{2,1,0:T(8,128)} %weights_ref.3, f32[2,512]{1,0:T(2,128)} %biases.1, ...), custom_call_target="tpu_custom_call" | custom-call | flops 9569304576 | bytes 6000000 | tf_op jit(solution)/shard_map/train_step/pallas_call | solution.py:705
  80.9 4.7 %clip_and_adamw.1 = (bf16[1352,128]{1,0:T(8,128)(2,1)}, bf16[1352,128]{1,0:T(8,128)(2,1)}, f32[1352,128]{1,0:T(8,128)}, f32[1,1]{1,0:T(1,128)}, f32[2,576,128]{2...) custom-call(bf16[1352,128]{1,0:T(8,128)(2,1)} %get-tuple-element.25., ...), custom_call_target="tpu_custom_call" | custom-call | flops 5000000 | bytes 7000000 | tf_op jit(solution)/shard_map/clip_and_adamw/pallas_call | solution.py:810

commit v4 on v3

--- a/solution.py
+++ b/solution.py
@@ -71,9 +71,10 @@
         self.piece = self.span // self.pieces
         self.groups = ((0, self.pieces // 2), (self.pieces // 2, self.pieces))
         self.wire = BF16 if self.own_in % 16 == 0 else F32
-        cut = (TAPS + 1) // 2 * self.out
-        self.parts = ((0, cut), (cut, self.cols))
+        self.line = self.major == 4
+        self.far_order = (2, 1, 3) if self.line else tuple(range(1, self.major))
         self.devices = self.dp * self.tensor
+        self.grant = (44 if self.wire == BF16 else 54) * 1024 * 1024
 
 
 def body(
@@ -115,15 +116,13 @@
     far_send,
     far_recv,
     shard,
-    rows_out,
     bias_sum,
     stats_all,
-    stats_t,
     local_sem,
-    out_sem,
-    wu_send,
-    wd_send,
+    ready,
+    wz_send,
     wz_recv,
+    wf_send,
     wy_send,
     wy_recv,
     ax_send,
@@ -180,20 +179,24 @@
 
     far_steps = range(1, sz.major)
     cross_steps = range(1, sz.pairs)
-    above, below = major + 1 < sz.major, major > 0
-    up, down = (2 * (major + 1) + minor, t), (2 * (major - 1) + minor, t)
+    middle = jnp.logical_and(major > 0, major < sz.major - 1)
+    far_steps = range(1, sz.major)
+    cross_steps = range(1, sz.pairs)
+    signal = functools.partial(pl.semaphore_signal, inc=1, device_id_type=MESH)
 
     barrier = pltpu.get_barrier_semaphore()
-
-    def greet(device):
-        pl.semaphore_signal(barrier, inc=1, device_id=device, device_id_type=MESH)
-
-    pl.when(above)(lambda: greet(up))
-    pl.when(below)(lambda: greet(down))
-    greet(near)
+    if sz.line:
+        pl.when(major > 0)(lambda: signal(barrier, device_id=(d - 2, t)))
+        pl.when(major < sz.major - 1)(lambda: signal(barrier, device_id=(d + 2, t)))
+        joined = jnp.where(middle, 2, 1) + 1 + sz.pairs
+    else:
+        for k in far_steps:
+            signal(barrier, device_id=far(k))
+        joined = sz.major + sz.pairs
+    signal(barrier, device_id=near)
     for k in cross_steps:
-        greet((d, cross_rank(k)))
-    greet(sibling)
+        signal(barrier, device_id=(d, cross_rank(k)))
+    signal(barrier, device_id=sibling)
 
     load_w = [pltpu.make_async_copy(weights_ref.at[l], w_in.at[l], local_sem.at[l]) for l in (0, 1)]
     load_frames = pltpu.make_async_copy(frames_ref, stage.at[0], local_sem.at[2])
@@ -203,68 +206,45 @@
     for copy in (load_w[0], load_frames, load_w[1], load_cot, load_biases, load_mask):
         copy.start()
 
-    def weight_block(l, part, slot):
-        first, last = sz.parts[part]
-        return w_all.at[l, slot, :, first:last]
-
-    def weight_up(l, part, source):
-        return same(
-            weight_block(l, part, 2 * source + minor), wu_send.at[l, part, source], wz_recv.at[l, part, source], up
-        )
-
-    def weight_down(l, part, source):
-        return same(
-            weight_block(l, part, 2 * source + minor), wd_send.at[l, part, source], wz_recv.at[l, part, source], down
-        )
-
-    def weight_over(l, part, source):
-        return same(
-            weight_block(l, part, 2 * source + minor), wy_send.at[l, part, source], wy_recv.at[l, part, source], near
-        )
-
-    def weights_out(l, part):
-        pl.when(above)(weight_up(l, part, major).start)
-        pl.when(below)(weight_down(l, part, major).start)
-
-    def weights_on(l, part):
-        @pl.loop(1, sz.major)
-        def _(step):
-            @pl.when(major - step >= 0)
-            def _():
-                source = major - step
-                weight_up(l, part, source).wait_recv()
-                pl.when(above)(weight_up(l, part, source).start)
-                weight_over(l, part, source).start()
-
-            @pl.when(major + step < sz.major)
-            def _():
-                source = major + step
-                weight_down(l, part, source).wait_recv()
-                pl.when(below)(weight_down(l, part, source).start)
-                weight_over(l, part, source).start()
-
-    def weights_here(l, part):
-        @pl.loop(0, sz.major)
-        def _(source):
-            same(
-                weight_block(l, part, 2 * source + 1 - minor),
-                wy_send.at[l, part, source],
-                wy_recv.at[l, part, source],
-                near,
-            ).wait_recv()
-
-    def weights_sent(l, part):
-        @pl.loop(0, sz.major)
-        def _(source):
-            weight_over(l, part, source).wait_send()
-
-            @pl.when(jnp.logical_and(source <= major, above))
-            def _():
-                weight_up(l, part, source).wait_send()
-
-            @pl.when(jnp.logical_and(source >= major, below))
-            def _():
-                weight_down(l, part, source).wait_send()
+    def weight_out(l, k):
+        return same(w_all.at[l, d], wz_send.at[l, k], wz_recv.at[l, k], far(k))
+
+    def weight_relay(l):
+        return same(w_all.at[l, far_slot(2)], wf_send.at[l], wz_recv.at[l, 3], far(1))
+
+    def weight_over(l, k):
+        return same(w_all.at[l, far_slot(k)], wy_send.at[l, k], wy_recv.at[l, k], near)
+
+    def weights_out(l):
+        for k in sz.far_order:
+            if sz.line and k == 3:
+                pl.when(middle)(weight_out(l, k).start)
+            else:
+                weight_out(l, k).start()
+
+    def weights_on(l, steps):
+        for k in steps:
+            same(w_all.at[l, far_slot(k)], wz_send.at[l, k], wz_recv.at[l, k], far(k)).wait_recv()
+            if sz.line and k == 2:
+                pl.when(middle)(weight_relay(l).start)
+            weight_over(l, k).start()
+
+    def weights_here(l):
+        for k in range(sz.major):
+            same(w_all.at[l, near_slot(k)], wy_send.at[l, k], wy_recv.at[l, k], near).wait_recv()
+
+    def weights_sent(l):
+        for k in range(sz.major):
+            weight_over(l, k).wait_send()
+            if sz.line and k == 3:
+
+                @pl.when(middle)
+                def _():
+                    weight_out(l, k).wait_send()
+                    weight_relay(l).wait_send()
+
+            elif k:
+                weight_out(l, k).wait_send()
 
     def round_weights(l):
         load_w[l].wait()
@@ -301,12 +281,11 @@
 
     whole = pl.ds(0, sz.span)
 
-    def product(l, part, maps, group):
+    def product(l, maps, group):
         rows = slice(group[0] * sz.piece, group[1] * sz.piece)
         left = jnp.concatenate([maps[q, rows] for q in range(sz.tensor)], axis=1)
-        first, last = sz.parts[part]
-        for start in range(first, last, WIDE):
-            stop = min(start + WIDE, last)
+        for start in range(0, sz.cols, WIDE):
+            stop = min(start + WIDE, sz.cols)
             right = w_all[l, :, :, start:stop].reshape(sz.chan, stop - start).astype(BF16)
             spread[sz.halo + rows.start : sz.halo + rows.stop, start:stop] = jnp.dot(
                 left, right, preferred_element_type=F32
@@ -466,15 +445,19 @@
         shard[...] = total
         squares = jnp.sum((total * total).reshape(sz.own_in // 8, 8, sz.cols), axis=0)
         for tap in range(TAPS):
-            rows_out[l, pl.ds(tap, sz.own_in, stride=TAPS), :] = shard[:, tap * sz.out : (tap + 1) * sz.out]
+            grads_out[l, pl.ds(tap, sz.own_in, stride=TAPS), :] = shard[:, tap * sz.out : (tap + 1) * sz.out]
         return sum(squares[:, tap * sz.out : (tap + 1) * sz.out] for tap in range(TAPS))
 
     round_weights(0)
-    joined = 1 + sz.pairs + above.astype(jnp.int32) + below.astype(jnp.int32)
     pl.semaphore_wait(barrier, joined)
-    for part in (0, 1):
-        weight_over(0, part, major).start()
-        weights_out(0, part)
+    if sz.line:
+
+        @pl.when(middle)
+        def _():
+            signal(ready, device_id=(d - 2, t))
+            signal(ready, device_id=(d + 2, t))
+
+    weight_over(0, 0).start()
     tail = sz.span - 16
     frames[t, tail:] = jnp.zeros((16, sz.out), BF16)
     load_frames.wait()
@@ -482,8 +465,10 @@
     for copy in gather_sends(0, frames, 0, whole):
         copy.start()
     round_weights(1)
-    for part in (0, 1):
-        weight_over(1, part, major).start()
+    weight_over(1, 0).start()
+    if sz.line:
+        pl.semaphore_wait(ready, 1)
+    weights_out(0)
 
     rest = sz.halo + sz.span
     for first in (0, rest):
@@ -510,48 +495,35 @@
     keep[...] = kept
 
     one, two = sz.groups
-    weights_on(0, 0)
-    for part in (0, 1):
-        weights_out(1, part)
+    weights_on(0, far_steps)
+    weights_out(1)
     gather_pass_on(0, frames, 0, whole)
-    weights_on(0, 1)
     gather_here(0, frames, 0, whole)
-    weights_here(0, 0)
-    product(0, 0, frames, one)
-    product(0, 0, frames, two)
-    weights_here(0, 1)
-    product(0, 1, frames, one)
+    weights_here(0)
+    weights_on(1, far_steps[:1])
+    product(0, frames, one)
     finish_four(0, one[1] - 1)
-    product(0, 1, frames, two)
+    weights_on(1, far_steps[1:2])
+    product(0, frames, two)
     finish_four(one[1] - 1, sz.pieces)
 
-    weights_on(1, 0)
-    stage[0] = acts[t, 0 : sz.real]
-    save_act4 = pltpu.make_async_copy(stage.at[0], act4_out, out_sem.at[0])
-    save_act4.start()
-    for p in range(*one):
-        gather_pass_on(1, acts, p, rows_of(p))
-    weights_on(1, 1)
-    for p in range(*two):
+    weights_on(1, far_steps[2:])
+    act4_out[...] = acts[t, 0 : sz.real]
+    for p in all_pieces:
         gather_pass_on(1, acts, p, rows_of(p))
     for p in all_pieces:
         gather_here(1, acts, p, rows_of(p))
-    weights_here(1, 0)
-    product(1, 0, acts, one)
-    product(1, 0, acts, two)
-    weights_here(1, 1)
-    product(1, 1, acts, one)
+    weights_here(1)
+    product(1, acts, one)
     finish_five(0, one[1] - 1)
-    product(1, 1, acts, two)
+    product(1, acts, two)
     finish_five(one[1] - 1, sz.pieces)
     spread_delta()
 
     grads_half(1, acts, True)
     back_products(1)
     grads_half(1, acts, False)
-    stage[1] = act5[0 : sz.real]
-    save_act5 = pltpu.make_async_copy(stage.at[1], act5_out, out_sem.at[1])
-    save_act5.start()
+    act5_out[...] = act5[0 : sz.real]
     for k in far_half:
         grads_far(1, k)
 
@@ -568,8 +540,6 @@
     for k in far_half:
         grads_far(0, k)
     squares = grads_done(1)
-    save_grads = [pltpu.make_async_copy(rows_out.at[l], grads_out.at[l], out_sem.at[3 + l]) for l in (0, 1)]
-    save_grads[1].start()
     for k in near_half:
         grads_far(0, k)
 
@@ -577,11 +547,9 @@
     def _(p):
         igrad[rows_of(p)] = back_total(0, p)
 
-    save_igrad = pltpu.make_async_copy(igrad.at[0 : sz.real], igrad_out, out_sem.at[2])
-    save_igrad.start()
+    igrad_out[...] = igrad[0 : sz.real]
 
     squares += grads_done(0)
-    save_grads[0].start()
 
     me = d * sz.tensor + t
     stats_all[me, 0:1, :] = jnp.sum(squares, axis=0, keepdims=True)
@@ -606,13 +574,10 @@
         total = stats_all[q]
         for slot in range(q + sz.tensor, sz.devices, sz.tensor):
             total += stats_all[slot]
-        stats_t[q] = total
-    save_stats = pltpu.make_async_copy(stats_t, stats_out, out_sem.at[5])
-    save_stats.start()
+        stats_out[q] = total
 
     for l in (0, 1):
-        for part in (0, 1):
-            weights_sent(l, part)
+        weights_sent(l)
         for k in far_steps:
             far_copy(l, k).wait_send()
         for k in range(sz.major):
@@ -633,9 +598,6 @@
     @pl.loop(1, sz.devices)
     def _(k):
         stats_copy(k, me).wait_send()
-
-    for copy in (save_act4, save_act5, save_igrad, *save_grads, save_stats):
-        copy.wait()
 
 
 def train_step(sz, frames, item_mask, weights, biases, cotangent):
@@ -671,17 +633,15 @@
         vmem((2, sz.major, *block), sz.wire),
         vmem((2, sz.major, *block), sz.wire),
         vmem(block, F32),
-        vmem((2, sz.rows, sz.out), F32),
         vmem((2, 8, sz.out), F32),
         vmem((sz.devices, 8, sz.out), F32),
-        vmem((sz.tensor, 8, sz.out), F32),
         sem((6,)),
-        sem((6,)),
-        sem((2, 2, sz.major)),
-        sem((2, 2, sz.major)),
-        sem((2, 2, sz.major)),
-        sem((2, 2, sz.major)),
-        sem((2, 2, sz.major)),
+        pltpu.SemaphoreType.REGULAR,
+        sem((2, sz.major)),
+        sem((2, sz.major)),
+        sem((2,)),
+        sem((2, sz.major)),
+        sem((2, sz.major)),
         sem((2, sz.pieces, sz.pairs)),
         sem((2, sz.pieces, sz.pairs)),
         sem((2, sz.pieces)),
@@ -699,42 +659,41 @@
         sem((sz.devices,)),
         sem((sz.devices,)),
     ]
-    anywhere = pl.BlockSpec(memory_space=pl.ANY)
     macs = 6 * sz.real * TAPS * sz.chan * sz.out
     rows = (sz.real, sz.out)
     return pl.pallas_call(
         functools.partial(body, sz),
         out_shape=[
-            jax.ShapeDtypeStruct(rows, BF16),
-            jax.ShapeDtypeStruct(rows, BF16),
-            jax.ShapeDtypeStruct(rows, F32),
-            jax.ShapeDtypeStruct((2, sz.rows, sz.out), F32),
-            jax.ShapeDtypeStruct((sz.tensor, 8, sz.out), F32),
+            vmem(rows, BF16),
+            vmem(rows, BF16),
+            vmem(rows, F32),
+            vmem((2, sz.rows, sz.out), F32),
+            vmem((sz.tensor, 8, sz.out), F32),
         ],
-        in_specs=[anywhere] * 5,
-        out_specs=[anywhere] * 5,
+        in_specs=[pl.BlockSpec(memory_space=pltpu.HBM)] * 5,
+        out_specs=[pl.BlockSpec(memory_space=vmem)] * 5,
         scratch_shapes=shapes,
         compiler_params=pltpu.CompilerParams(
-            collective_id=0, has_side_effects=True, vmem_limit_bytes=60 * 1024 * 1024
+            collective_id=0, has_side_effects=True, vmem_limit_bytes=sz.grant
         ),
         cost_estimate=pl.CostEstimate(flops=2 * macs, bytes_accessed=6_000_000, transcendentals=0),
         name="train_step",
-    )(frames, item_mask, weights, biases, cotangent)
+    )(*(pltpu.with_memory_space_constraint(x, pltpu.HBM) for x in (frames, item_mask, weights, biases, cotangent)))
 
 
 def finish_body(
     sz,
-    act4_ref,
-    act5_ref,
-    igrad_ref,
-    grads_ref,
-    stats_ref,
-    weights_ref,
-    first_ref,
-    second_ref,
-    biases,
-    bias_first,
-    bias_second,
+    act4,
+    act5,
+    igrad,
+    grads,
+    stats,
+    weights,
+    first,
+    second,
+    biases_ref,
+    bias_first_ref,
+    bias_second_ref,
     act4_out,
     act5_out,
     igrad_out,
@@ -745,36 +704,27 @@
     biases_out,
     bias_first_out,
     bias_second_out,
-    stats,
-    maps,
-    igrad,
     olds,
     news,
     in_sem,
     out_sem,
     move_sem,
 ):
-    sources = (weights_ref, grads_ref, first_ref, second_ref)
     targets = (weights_out, first_out, second_out)
-    loads = [
-        [pltpu.make_async_copy(ref.at[l], olds.at[l, i], in_sem.at[l, i]) for i, ref in enumerate(sources)]
-        for l in (0, 1)
-    ]
     stores = [
         [pltpu.make_async_copy(news.at[l, i], ref.at[l], out_sem.at[l, i]) for i, ref in enumerate(targets)]
         for l in (0, 1)
     ]
-    moves = (
-        (act4_ref, maps.at[0], act4_out),
-        (act5_ref, maps.at[1], act5_out),
-        (igrad_ref, igrad, igrad_out),
-    )
-    moves_in = [pltpu.make_async_copy(src, held, move_sem.at[0, i]) for i, (src, held, _) in enumerate(moves)]
-    moves_out = [pltpu.make_async_copy(held, dst, move_sem.at[1, i]) for i, (_, held, dst) in enumerate(moves)]
-    load_stats = pltpu.make_async_copy(stats_ref, stats, move_sem.at[0, 3])
-    for copy in (load_stats, *loads[0], *moves_in, *loads[1]):
+    moves = [
+        pltpu.make_async_copy(held, ref, move_sem.at[i])
+        for i, (held, ref) in enumerate(((act4, act4_out), (act5, act5_out), (igrad, igrad_out)))
+    ]
+    loads = [
+        pltpu.make_async_copy(ref, olds.at[i], in_sem.at[i])
+        for i, ref in enumerate((biases_ref, bias_first_ref, bias_second_ref))
+    ]
+    for copy in (*loads, *moves):
         copy.start()
-    load_stats.wait()
     bias_grad = jnp.concatenate([stats[q, 1:3, :] for q in range(sz.tensor)], axis=1)
     squares = jnp.sum(stats[:, 0, :], axis=(0, 1), keepdims=True) + jnp.sum(
         bias_grad * bias_grad, axis=(0, 1), keepdims=True
@@ -782,31 +732,28 @@
     grad_norm = jnp.sqrt(squares)
     factor = jnp.minimum(1.0, CLIP_NORM / (grad_norm + 1e-06))
     norm_out[...] = grad_norm
-    biases_out[...], bias_first_out[...], bias_second_out[...] = adam_update(
-        biases[...], bias_grad * factor, bias_first[...], bias_second[...], BIAS_RATE, 0.0
-    )
     for l in (0, 1):
-        for copy in loads[l]:
-            copy.wait()
         news[l, 0], news[l, 1], news[l, 2] = adam_update(
-            olds[l, 0], olds[l, 1] * factor, olds[l, 2], olds[l, 3], RATE, DECAY
+            weights[l], grads[l] * factor, first[l], second[l], RATE, DECAY
         )
         for copy in stores[l]:
             copy.start()
-        if l == 0:
-            for here, there in zip(moves_in, moves_out):
-                here.wait()
-                there.start()
-    for copy in (*stores[0], *stores[1], *moves_out):
+    for copy in loads:
         copy.wait()
+    biases_out[...], bias_first_out[...], bias_second_out[...] = adam_update(
+        olds[0], bias_grad * factor, olds[1], olds[2], BIAS_RATE, 0.0
+    )
+    for copy in (*moves, *stores[0], *stores[1]):
+        copy.wait()
 
 
 def finish(sz, act4, act5, igrad, grads, stats, weights, first, second, biases, bias_first, bias_second):
-    anywhere = pl.BlockSpec(memory_space=pl.ANY)
     inside = pl.BlockSpec(memory_space=pltpu.VMEM)
     outside = pl.BlockSpec(memory_space=pltpu.HBM)
     like = lambda x: jax.ShapeDtypeStruct(x.shape, x.dtype)
     sem = pltpu.SemaphoreType.DMA
+    held = [pltpu.with_memory_space_constraint(x, pltpu.VMEM) for x in (act4, act5, igrad, grads, stats, weights, first, second)]
+    given = [pltpu.with_memory_space_constraint(x, pltpu.HBM) for x in (biases, bias_first, bias_second)]
     return pl.pallas_call(
         functools.partial(finish_body, sz),
         out_shape=[
@@ -821,22 +768,19 @@
             like(bias_first),
             like(bias_second),
         ],
-        in_specs=[outside] * 5 + [anywhere] * 3 + [inside] * 3,
+        in_specs=[inside] * 8 + [outside] * 3,
         out_specs=[outside] * 3 + [inside] + [outside] * 3 + [inside] * 3,
         scratch_shapes=[
-            pltpu.VMEM((sz.tensor, 8, sz.out), F32),
-            pltpu.VMEM((2, sz.real, sz.out), BF16),
-            pltpu.VMEM((sz.real, sz.out), F32),
-            pltpu.VMEM((2, 4, sz.rows, sz.out), F32),
+            pltpu.VMEM((3, *biases.shape), F32),
             pltpu.VMEM((2, 3, sz.rows, sz.out), F32),
-            sem((2, 4)),
+            sem((3,)),
             sem((2, 3)),
-            sem((2, 4)),
+            sem((3,)),
         ],
-        compiler_params=pltpu.CompilerParams(vmem_limit_bytes=60 * 1024 * 1024),
+        compiler_params=pltpu.CompilerParams(vmem_limit_bytes=8 * 1024 * 1024),
         cost_estimate=pl.CostEstimate(flops=5_000_000, bytes_accessed=7_000_000, transcendentals=0),
         name="clip_and_adamw",
-    )(act4, act5, igrad, grads, stats, weights, first, second, biases, bias_first, bias_second)
+    )(*held, *given)
 
 
 def on_device(

time: 85.8 us -> 83.9 us (0.978)
  Pallas kernels: 85 us -> 82.8 us
    pallas_call x1, Pallas kernels: 4.73 us -> 2.8 us  [finish(): pl.pallas_call(functools.partial(finish_body, sz), out_shape=[like(act4),...]
where the time goes in v4:
time: 83.9 us; the launch traced here: 83.7 us
  Pallas kernels  82.8 us (99%)
  between operations  0.86 us (1%)
    pallas_call x1, Pallas kernels, train_step(): pl.pallas_call(functools.partial(body, sz), out_shape=[vmem(rows, BF16),...  80 us
    pallas_call x1, Pallas kernels, finish(): pl.pallas_call(functools.partial(finish_body, sz), out_shape=[like(act4),...  2.8 us

profile of v4, /device:TPU:0, one launch (start us, length us, event | category | flops | bytes accessed | tf_op | source)
XLA Modules:
  0.0 83.7 jit_solution(7488870234051256257)
XLA Ops:
  0.6 0.0 copy-start
  0.7 0.0 copy-start.1
  0.7 0.0 copy-start.2
  0.7 80.0 %train_step.1 = (bf16[1352,128]{1,0:T(8,128)(2,1)S(1)}, bf16[1352,128]{1,0:T(8,128)(2,1)S(1)}, f32[1352,128]{1,0:T(8,128)S(1)}, f32[2,576,128]{2,1,0:T(8,128)S(1)}, f32[4,8,128]{2,1,0:T(8,128)S(1)}) custom-call(bf16[1352,128]{1,0:T(8,128)(2,1)} %bitcast.17, s32[8]{0:T(128)} %mask_ref.1, f32[2,576,128]{2,1,0:T(8,128)} %weights.1, f32[2,512]{1,0:T(2,128)} %biases_ref.3, ...), custom_call_target="tpu_custom_call" | custom-call | flops 9569304576 | bytes 6000000 | tf_op jit(solution)/shard_map/train_step/pallas_call | solution.py:664
  80.7 0.0 copy-done
  80.7 0.0 copy-done.1
  80.7 0.0 copy-done.2
  80.7 2.8 %clip_and_adamw.1 = (bf16[1352,128]{1,0:T(8,128)(2,1)}, bf16[1352,128]{1,0:T(8,128)(2,1)}, f32[1352,128]{1,0:T(8,128)}, f32[1,1]{1,0:T(1,128)}, f32[2,576,128]{2...) custom-call(bf16[1352,128]{1,0:T(8,128)(2,1)S(1)} %get-tuple-element, ...), custom_call_target="tpu_custom_call" | custom-call | flops 5000000 | bytes 7000000 | tf_op jit(solution)/shard_map/clip_and_adamw/pallas_call | solution.py:757
Async XLA Ops:
  0.6 80.0 %copy-start = (f32[2,576,128]{2,1,0:T(8,128)S(1)}, f32[2,576,128]{2,1,0:T(8,128)}, u32[]{:S(2)}) copy-start(f32[2,576,128]{2,1,0:T(8,128)} %weights.1) | copy-start | bytes 1769476
  0.7 80.0 %copy-start.1 = (f32[2,576,128]{2,1,0:T(8,128)S(1)}, f32[2,576,128]{2,1,0:T(8,128)}, u32[]{:S(2)}) copy-start(f32[2,576,128]{2,1,0:T(8,128)} %first.1) | copy-start | bytes 1769476
  0.7 80.0 %copy-start.2 = (f32[2,576,128]{2,1,0:T(8,128)S(1)}, f32[2,576,128]{2,1,0:T(8,128)}, u32[]{:S(2)}) copy-start(f32[2,576,128]{2,1,0:T(8,128)} %second.1) | copy-start | bytes 1769476

commit v5 on v4

--- a/solution.py
+++ b/solution.py
@@ -74,6 +74,8 @@
         self.line = self.major == 4
         self.far_order = (2, 1, 3) if self.line else tuple(range(1, self.major))
         self.devices = self.dp * self.tensor
+        self.shares = 2 if self.own_in % 32 == 0 else 1
+        self.share = self.own_in // self.shares
         self.grant = (44 if self.wire == BF16 else 54) * 1024 * 1024
 
 
@@ -115,6 +117,7 @@
     near_recv,
     far_send,
     far_recv,
+    relay_recv,
     shard,
     bias_sum,
     stats_all,
@@ -139,6 +142,7 @@
     gy_recv,
     gz_send,
     gz_recv,
+    gr_recv,
     st_send,
     st_recv,
 ):
@@ -391,12 +395,14 @@
                 cross_send[l, k, rows_of(p)] = total.astype(BF16)
                 cross_copy(l, p, k).start()
 
-    def back_products(l):
+    def back_products(l, between=None):
         one, two = sz.groups
         back_to_sibling(l, one)
         back_own(l, one)
         back_to_sibling(l, two)
         back_across(l, one)
+        if between:
+            between()
         back_own(l, two)
         back_across(l, two)
 
@@ -407,46 +413,104 @@
             total += cross_recv[l, k, rows_of(p)].astype(F32)
         return total
 
-    def near_copy(l, k):
-        return remote(near_send.at[l, k], near_recv.at[l, k], gy_send.at[l, k], gy_recv.at[l, k], near)
-
-    def far_copy(l, k):
-        return remote(far_send.at[l, k], far_recv.at[l, k], gz_send.at[l, k], gz_recv.at[l, k], far(k))
+    shares = range(sz.shares)
+
+    def share_of(h):
+        return slice(h * sz.share, (h + 1) * sz.share)
+
+    def near_copy(l, k, h):
+        return remote(
+            near_send.at[l, k, share_of(h)],
+            near_recv.at[l, k, share_of(h)],
+            gy_send.at[l, k, h],
+            gy_recv.at[l, k, h],
+            near,
+        )
+
+    def far_copy(l, k, h):
+        return remote(
+            far_send.at[l, k, share_of(h)],
+            far_recv.at[l, k, share_of(h)],
+            gz_send.at[l, k, h],
+            gz_recv.at[l, k, h],
+            far(k),
+        )
 
     half = sz.tensor // 2
-    far_half = [k for k in far_steps if k >= sz.major // 2]
+    far_half = [k for k in reversed(far_steps) if k >= sz.major // 2]
     near_half = [k for k in far_steps if k < sz.major // 2]
 
-    def grads_half(l, maps, other):
-        own = lax.div(major, sz.major // 2)
-        first = (1 - own if other else own) * half
-        left = jnp.concatenate([maps[first + q] for q in range(half)], axis=1)
-        into = pl.ds(first * sz.slots, half * sz.slots)
+    def grads_block(l, maps, block, width, steps):
+        left = jnp.concatenate([maps[block + q] for q in range(width)], axis=1)
+        into = pl.ds(block * sz.slots, width * sz.slots)
         for start in range(0, sz.cols, WIDE):
             stop = min(start + WIDE, sz.cols)
-            product = lax.dot_general(left, deltas[:, start:stop], (((0,), (0,)), ((), ())), preferred_element_type=F32)
-            kgrad[l, into, :, start:stop] = product.reshape(half * sz.slots, sz.own_in, stop - start)
-        for k in far_half if other else [*near_half, 0]:
+            product = lax.dot_general(
+                left, deltas[:, start:stop], (((0,), (0,)), ((), ())), preferred_element_type=F32
+            )
+            kgrad[l, into, :, start:stop] = product.reshape(width * sz.slots, sz.own_in, stop - start)
+        for k in steps:
             near_send[l, k] = kgrad[l, near_slot(k)].astype(sz.wire)
-            near_copy(l, k).start()
+            for h in shares:
+                near_copy(l, k, h).start()
+
+    own_half = lax.div(major, sz.major // 2)
+
+    def grads_half(l, maps, other):
+        first = (1 - own_half if other else own_half) * half
+        grads_block(l, maps, first, half, far_half if other else [*near_half, 0])
+
+    def grads_place(l, maps, k):
+        grads_block(l, maps, flip_bits(major, k), 1, [k])
+
+    def relay_copy(l, h):
+        rows = share_of(h)
+        return remote(
+            far_send.at[l, 3, rows], relay_recv.at[l, rows], gz_send.at[l, 3, h], gr_recv.at[l, h], far(1)
+        )
 
     def grads_far(l, k):
-        near_copy(l, k).wait_recv()
-        far_send[l, k] = (kgrad[l, far_slot(k)] + near_recv[l, k].astype(F32)).astype(sz.wire)
-        far_copy(l, k).start()
-
-    def grads_done(l):
-        near_copy(l, 0).wait_recv()
-        for k in far_steps:
-            far_copy(l, k).wait_recv()
+        for h in shares:
+            rows = share_of(h)
+            near_copy(l, k, h).wait_recv()
+            total = kgrad[l, far_slot(k), rows] + near_recv[l, k, rows].astype(F32)
+            if sz.line and k == 2:
+
+                @pl.when(middle)
+                def _():
+                    relay_copy(l, h).wait_recv()
+                    far_send[l, k, rows] = (total + relay_recv[l, rows].astype(F32)).astype(sz.wire)
+
+                @pl.when(jnp.logical_not(middle))
+                def _():
+                    far_send[l, k, rows] = total.astype(sz.wire)
+
+            else:
+                far_send[l, k, rows] = total.astype(sz.wire)
+            if sz.line and k == 3:
+                pl.when(middle)(far_copy(l, k, h).start)
+                pl.when(jnp.logical_not(middle))(relay_copy(l, h).start)
+            else:
+                far_copy(l, k, h).start()
+
+    def grads_sum(l):
+        for h in shares:
+            near_copy(l, 0, h).wait_recv()
+            for k in far_steps:
+                if sz.line and k == 3:
+                    pl.when(middle)(far_copy(l, k, h).wait_recv)
+                else:
+                    far_copy(l, k, h).wait_recv()
         total = kgrad[l, d] + near_recv[l, 0].astype(F32)
         for k in far_steps:
             total += far_recv[l, k].astype(F32)
         shard[...] = total
         squares = jnp.sum((total * total).reshape(sz.own_in // 8, 8, sz.cols), axis=0)
+        return sum(squares[:, tap * sz.out : (tap + 1) * sz.out] for tap in range(TAPS))
+
+    def grads_out_rows(l):
         for tap in range(TAPS):
             grads_out[l, pl.ds(tap, sz.own_in, stride=TAPS), :] = shard[:, tap * sz.out : (tap + 1) * sz.out]
-        return sum(squares[:, tap * sz.out : (tap + 1) * sz.out] for tap in range(TAPS))
 
     round_weights(0)
     pl.semaphore_wait(barrier, joined)
@@ -482,6 +546,12 @@
             edges[e, first : first + sz.items, :] = nothing
     edges[2, sz.real :, :] = jnp.zeros((sz.span - sz.real, sz.out), F32)
     bias_sum[...] = jnp.zeros_like(bias_sum)
+    if sz.line:
+
+        @pl.when(jnp.logical_not(middle))
+        def _():
+            far_recv[:, 3] = jnp.zeros((2, sz.own_in, sz.cols), sz.wire)
+
 
     cot[tail:] = jnp.zeros((16, sz.out), BF16)
     load_cot.wait()
@@ -520,28 +590,36 @@
     finish_five(one[1] - 1, sz.pieces)
     spread_delta()
 
-    grads_half(1, acts, True)
-    back_products(1)
+    if sz.line and sz.tensor == sz.major:
+        grads_place(1, acts, 3)
+        back_products(1, lambda: grads_place(1, acts, 2))
+    else:
+        grads_half(1, acts, True)
+        back_products(1)
     grads_half(1, acts, False)
     act5_out[...] = act5[0 : sz.real]
-    for k in far_half:
-        grads_far(1, k)
+    grads_far(1, far_half[0])
 
     @pl.loop(0, sz.pieces)
     def _(p):
         note_delta(0, p, (back_total(1, p) * slope4[rows_of(p)]).astype(BF16).astype(F32))
 
     spread_delta()
-    grads_half(0, frames, True)
+    if sz.line and sz.tensor == sz.major:
+        grads_place(0, frames, 3)
+        grads_place(0, frames, 2)
+    else:
+        grads_half(0, frames, True)
+    for k in far_half[1:]:
+        grads_far(1, k)
+    grads_half(0, frames, False)
     for k in near_half:
         grads_far(1, k)
-    grads_half(0, frames, False)
-    back_products(0)
-    for k in far_half:
+    back_products(0, lambda: grads_far(0, far_half[0]))
+    for k in (*far_half[1:], *near_half):
         grads_far(0, k)
-    squares = grads_done(1)
-    for k in near_half:
-        grads_far(0, k)
+    squares = grads_sum(1)
+    grads_out_rows(1)
 
     @pl.loop(0, sz.pieces)
     def _(p):
@@ -549,39 +627,35 @@
 
     igrad_out[...] = igrad[0 : sz.real]
 
-    squares += grads_done(0)
+    squares += grads_sum(0)
 
     me = d * sz.tensor + t
     stats_all[me, 0:1, :] = jnp.sum(squares, axis=0, keepdims=True)
     for l in (0, 1):
         stats_all[me, l + 1 : l + 2, :] = jnp.sum(bias_sum[l], axis=0, keepdims=True)
-    stats_all[me, 3:8, :] = jnp.zeros((5, sz.out), F32)
 
     def stats_copy(k, slot):
         other = lax.rem(me + k, sz.devices)
         device = (lax.div(other, sz.tensor), lax.rem(other, sz.tensor))
-        return same(stats_all.at[slot], st_send.at[k], st_recv.at[k], device)
-
-    @pl.loop(1, sz.devices)
-    def _(k):
-        stats_copy(k, me).start()
-
-    @pl.loop(1, sz.devices)
-    def _(k):
-        stats_copy(k, lax.rem(me + sz.devices - k, sz.devices)).wait_recv()
-
-    for q in range(sz.tensor):
-        total = stats_all[q]
-        for slot in range(q + sz.tensor, sz.devices, sz.tensor):
-            total += stats_all[slot]
-        stats_out[q] = total
-
+        return same(stats_all.at[slot, 0:3], st_send.at[k], st_recv.at[k], device)
+
+    def each_device(act):
+        if sz.devices <= 32:
+            for k in range(1, sz.devices):
+                act(k)
+        else:
+            pl.loop(1, sz.devices)(act)
+
+    each_device(lambda k: stats_copy(k, me).start())
+
+    grads_out_rows(0)
     for l in (0, 1):
         weights_sent(l)
-        for k in far_steps:
-            far_copy(l, k).wait_send()
-        for k in range(sz.major):
-            near_copy(l, k).wait_send()
+        for h in shares:
+            for k in far_steps:
+                far_copy(l, k, h).wait_send()
+            for k in range(sz.major):
+                near_copy(l, k, h).wait_send()
 
         @pl.loop(0, sz.pieces)
         def _(p):
@@ -595,9 +669,15 @@
     def _(p):
         gather_sent(1, acts, p, rows_of(p))
 
-    @pl.loop(1, sz.devices)
-    def _(k):
-        stats_copy(k, me).wait_send()
+    each_device(lambda k: stats_copy(k, lax.rem(me + sz.devices - k, sz.devices)).wait_recv())
+
+    for q in range(sz.tensor):
+        total = stats_all[q, 0:3]
+        for slot in range(q + sz.tensor, sz.devices, sz.tensor):
+            total += stats_all[slot, 0:3]
+        stats_out[q, 0:3] = total
+
+    each_device(lambda k: stats_copy(k, me).wait_send())
 
 
 def train_step(sz, frames, item_mask, weights, biases, cotangent):
@@ -632,6 +712,7 @@
         vmem((2, sz.major, *block), sz.wire),
         vmem((2, sz.major, *block), sz.wire),
         vmem((2, sz.major, *block), sz.wire),
+        vmem((2, *block), sz.wire),
         vmem(block, F32),
         vmem((2, 8, sz.out), F32),
         vmem((sz.devices, 8, sz.out), F32),
@@ -652,10 +733,11 @@
         sem((2, sz.pieces)),
         sem((2, sz.pieces, sz.pairs)),
         sem((2, sz.pieces, sz.pairs)),
-        sem((2, sz.major)),
-        sem((2, sz.major)),
-        sem((2, sz.major)),
-        sem((2, sz.major)),
+        sem((2, sz.major, sz.shares)),
+        sem((2, sz.major, sz.shares)),
+        sem((2, sz.major, sz.shares)),
+        sem((2, sz.major, sz.shares)),
+        sem((2, sz.shares)),
         sem((sz.devices,)),
         sem((sz.devices,)),
     ]
@@ -711,9 +793,12 @@
     move_sem,
 ):
     targets = (weights_out, first_out, second_out)
+    parts = [(l, pl.ds(r * sz.rows // 2, sz.rows // 2)) for l in (0, 1) for r in (0, 1)]
+    if sz.rows % 16:
+        parts = [(l, pl.ds(0, sz.rows)) for l in (0, 1)]
     stores = [
-        [pltpu.make_async_copy(news.at[l, i], ref.at[l], out_sem.at[l, i]) for i, ref in enumerate(targets)]
-        for l in (0, 1)
+        [pltpu.make_async_copy(news.at[l, i, r], ref.at[l, r], out_sem.at[p, i]) for i, ref in enumerate(targets)]
+        for p, (l, r) in enumerate(parts)
     ]
     moves = [
         pltpu.make_async_copy(held, ref, move_sem.at[i])
@@ -732,18 +817,18 @@
     grad_norm = jnp.sqrt(squares)
     factor = jnp.minimum(1.0, CLIP_NORM / (grad_norm + 1e-06))
     norm_out[...] = grad_norm
-    for l in (0, 1):
-        news[l, 0], news[l, 1], news[l, 2] = adam_update(
-            weights[l], grads[l] * factor, first[l], second[l], RATE, DECAY
+    for p, (l, r) in enumerate(parts):
+        news[l, 0, r], news[l, 1, r], news[l, 2, r] = adam_update(
+            weights[l, r], grads[l, r] * factor, first[l, r], second[l, r], RATE, DECAY
         )
-        for copy in stores[l]:
+        for copy in stores[p]:
             copy.start()
     for copy in loads:
         copy.wait()
     biases_out[...], bias_first_out[...], bias_second_out[...] = adam_update(
         olds[0], bias_grad * factor, olds[1], olds[2], BIAS_RATE, 0.0
     )
-    for copy in (*moves, *stores[0], *stores[1]):
+    for copy in (*moves, *(copy for part in stores for copy in part)):
         copy.wait()
 
 
@@ -774,7 +859,7 @@
             pltpu.VMEM((3, *biases.shape), F32),
             pltpu.VMEM((2, 3, sz.rows, sz.out), F32),
             sem((3,)),
-            sem((2, 3)),
+            sem((4, 3)),
             sem((3,)),
         ],
         compiler_params=pltpu.CompilerParams(vmem_limit_bytes=8 * 1024 * 1024),

time: 83.9 us -> 82.6 us (0.985)
  Pallas kernels: 82.8 us -> 81.6 us
    pallas_call x1, Pallas kernels: 80 us -> 78.8 us  [train_step(): pl.pallas_call(functools.partial(body, sz), out_shape=[vmem(rows, BF16),...]
where the time goes in v5:
time: 82.6 us; the launch traced here: 82.4 us
  Pallas kernels  81.6 us (99%)
  between operations  0.86 us (1%)
    pallas_call x1, Pallas kernels, train_step(): pl.pallas_call(functools.partial(body, sz), out_shape=[vmem(rows, BF16),...  78.8 us
    pallas_call x1, Pallas kernels, finish(): pl.pallas_call(functools.partial(finish_body, sz), out_shape=[like(act4),...  2.79 us

profile of v5, /device:TPU:0, one launch (start us, length us, event | category | flops | bytes accessed | tf_op | source)
XLA Modules:
  0.0 82.4 jit_solution(4272142058775552481)
XLA Ops:
  0.6 0.0 copy-start
  0.7 0.0 copy-start.1
  0.7 0.0 copy-start.2
  0.7 78.8 %train_step.1 = (bf16[1352,128]{1,0:T(8,128)(2,1)S(1)}, bf16[1352,128]{1,0:T(8,128)(2,1)S(1)}, f32[1352,128]{1,0:T(8,128)S(1)}, f32[2,576,128]{2,1,0:T(8,128)S(1)}, f32[4,8,128]{2,1,0:T(8,128)S(1)}) custom-call(bf16[1352,128]{1,0:T(8,128)(2,1)} %bitcast.17, s32[8]{0:T(128)} %mask_ref.1, f32[2,576,128]{2,1,0:T(8,128)} %weights.1, f32[2,512]{1,0:T(2,128)} %biases_ref.3, ...), custom_call_target="tpu_custom_call" | custom-call | flops 9569304576 | bytes 6000000 | tf_op jit(solution)/shard_map/train_step/pallas_call | solution.py:746
  79.5 0.0 copy-done
  79.5 0.0 copy-done.1
  79.5 0.0 copy-done.2
  79.5 2.8 %clip_and_adamw.1 = (bf16[1352,128]{1,0:T(8,128)(2,1)}, bf16[1352,128]{1,0:T(8,128)(2,1)}, f32[1352,128]{1,0:T(8,128)}, f32[1,1]{1,0:T(1,128)}, f32[2,576,128]{2...) custom-call(bf16[1352,128]{1,0:T(8,128)(2,1)S(1)} %get-tuple-element, ...), custom_call_target="tpu_custom_call" | custom-call | flops 5000000 | bytes 7000000 | tf_op jit(solution)/shard_map/clip_and_adamw/pallas_call | solution.py:842
Async XLA Ops:
  0.6 78.8 %copy-start = (f32[2,576,128]{2,1,0:T(8,128)S(1)}, f32[2,576,128]{2,1,0:T(8,128)}, u32[]{:S(2)}) copy-start(f32[2,576,128]{2,1,0:T(8,128)} %weights.1) | copy-start | bytes 1769476
  0.7 78.8 %copy-start.1 = (f32[2,576,128]{2,1,0:T(8,128)S(1)}, f32[2,576,128]{2,1,0:T(8,128)}, u32[]{:S(2)}) copy-start(f32[2,576,128]{2,1,0:T(8,128)} %first.1) | copy-start | bytes 1769476
  0.7 78.8 %copy-start.2 = (f32[2,576,128]{2,1,0:T(8,128)S(1)}, f32[2,576,128]{2,1,0:T(8,128)}, u32[]{:S(2)}) copy-start(f32[2,576,128]{2,1,0:T(8,128)} %second.1) | copy-start | bytes 1769476

commit v6 on v5

--- a/solution.py
+++ b/solution.py
@@ -73,6 +73,8 @@
         self.wire = BF16 if self.own_in % 16 == 0 else F32
         self.line = self.major == 4
         self.far_order = (2, 1, 3) if self.line else tuple(range(1, self.major))
+        cut = (TAPS + 1) // 2 * self.out
+        self.parts = (((0, cut), (cut, self.cols)), ((0, self.cols),))
         self.devices = self.dp * self.tensor
         self.shares = 2 if self.own_in % 32 == 0 else 1
         self.share = self.own_in // self.shares
@@ -216,8 +218,14 @@
     def weight_relay(l):
         return same(w_all.at[l, far_slot(2)], wf_send.at[l], wz_recv.at[l, 3], far(1))
 
-    def weight_over(l, k):
-        return same(w_all.at[l, far_slot(k)], wy_send.at[l, k], wy_recv.at[l, k], near)
+    def weight_over(l, k, part):
+        first, last = sz.parts[l][part]
+        block = w_all.at[l, far_slot(k), :, first:last]
+        return same(block, wy_send.at[l, k, part], wy_recv.at[l, k, part], near)
+
+    def weights_over(l, k):
+        for part in range(len(sz.parts[l])):
+            weight_over(l, k, part).start()
 
     def weights_out(l):
         for k in sz.far_order:
@@ -231,15 +239,18 @@
             same(w_all.at[l, far_slot(k)], wz_send.at[l, k], wz_recv.at[l, k], far(k)).wait_recv()
             if sz.line and k == 2:
                 pl.when(middle)(weight_relay(l).start)
-            weight_over(l, k).start()
-
-    def weights_here(l):
+            weights_over(l, k)
+
+    def weights_here(l, part):
+        first, last = sz.parts[l][part]
         for k in range(sz.major):
-            same(w_all.at[l, near_slot(k)], wy_send.at[l, k], wy_recv.at[l, k], near).wait_recv()
+            block = w_all.at[l, near_slot(k), :, first:last]
+            same(block, wy_send.at[l, k, part], wy_recv.at[l, k, part], near).wait_recv()
 
     def weights_sent(l):
         for k in range(sz.major):
-            weight_over(l, k).wait_send()
+            for part in range(len(sz.parts[l])):
+                weight_over(l, k, part).wait_send()
             if sz.line and k == 3:
 
                 @pl.when(middle)
@@ -285,11 +296,12 @@
 
     whole = pl.ds(0, sz.span)
 
-    def product(l, maps, group):
+    def product(l, part, maps, group):
         rows = slice(group[0] * sz.piece, group[1] * sz.piece)
         left = jnp.concatenate([maps[q, rows] for q in range(sz.tensor)], axis=1)
-        for start in range(0, sz.cols, WIDE):
-            stop = min(start + WIDE, sz.cols)
+        first, last = sz.parts[l][part]
+        for start in range(first, last, WIDE):
+            stop = min(start + WIDE, last)
             right = w_all[l, :, :, start:stop].reshape(sz.chan, stop - start).astype(BF16)
             spread[sz.halo + rows.start : sz.halo + rows.stop, start:stop] = jnp.dot(
                 left, right, preferred_element_type=F32
@@ -318,15 +330,13 @@
         shifted[1, rows] = delta
         shifted[2, rows] = delta * edges[1, rows_of(p)]
 
-    def spread_delta():
-        @pl.loop(0, sz.pieces)
-        def _(p):
-            for a in range(3):
-                for b in range(3):
-                    shift = sz.items * (sz.width * (a - 1) + b - 1)
-                    tap = 3 * a + b
-                    rows = pl.ds(pl.multiple_of(p * sz.piece + sz.halo - shift, 8), sz.piece)
-                    deltas[rows_of(p), tap * sz.out : (tap + 1) * sz.out] = shifted[b, rows].astype(BF16)
+    def spread_delta(p):
+        for a in range(3):
+            for b in range(3):
+                shift = sz.items * (sz.width * (a - 1) + b - 1)
+                tap = 3 * a + b
+                rows = pl.ds(pl.multiple_of(p * sz.piece + sz.halo - shift, 8), sz.piece)
+                deltas[rows_of(p), tap * sz.out : (tap + 1) * sz.out] = shifted[b, rows].astype(BF16)
 
     def finish_four(first, last):
         @pl.loop(first, last)
@@ -347,6 +357,7 @@
             act5[rows_of(p)] = by_item(act).astype(BF16)
             delta = (by_item(cot[rows_of(p)].astype(F32)) * slope).astype(BF16).astype(F32)
             note_delta(1, p, delta)
+            pl.when(p > 0)(lambda: spread_delta(p - 1))
 
     def part_copy(l, p):
         rows = rows_of(p)
@@ -395,16 +406,13 @@
                 cross_send[l, k, rows_of(p)] = total.astype(BF16)
                 cross_copy(l, p, k).start()
 
-    def back_products(l, between=None):
-        one, two = sz.groups
-        back_to_sibling(l, one)
-        back_own(l, one)
-        back_to_sibling(l, two)
-        back_across(l, one)
-        if between:
-            between()
-        back_own(l, two)
-        back_across(l, two)
+    def back_products(l, first=None, second=None):
+        for group, meanwhile in zip(sz.groups, (first, second)):
+            back_to_sibling(l, group)
+            if meanwhile:
+                meanwhile()
+            back_own(l, group)
+            back_across(l, group)
 
     def back_total(l, p):
         total = part_own[pair, rows_of(p)] + part_recv[l, pair, rows_of(p)].astype(F32)
@@ -521,7 +529,7 @@
             signal(ready, device_id=(d - 2, t))
             signal(ready, device_id=(d + 2, t))
 
-    weight_over(0, 0).start()
+    weights_over(0, 0)
     tail = sz.span - 16
     frames[t, tail:] = jnp.zeros((16, sz.out), BF16)
     load_frames.wait()
@@ -529,7 +537,7 @@
     for copy in gather_sends(0, frames, 0, whole):
         copy.start()
     round_weights(1)
-    weight_over(1, 0).start()
+    weights_over(1, 0)
     if sz.line:
         pl.semaphore_wait(ready, 1)
     weights_out(0)
@@ -569,30 +577,33 @@
     weights_out(1)
     gather_pass_on(0, frames, 0, whole)
     gather_here(0, frames, 0, whole)
-    weights_here(0)
+    weights_here(0, 0)
+    product(0, 0, frames, one)
+    product(0, 0, frames, two)
+    weights_here(0, 1)
     weights_on(1, far_steps[:1])
-    product(0, frames, one)
+    product(0, 1, frames, one)
     finish_four(0, one[1] - 1)
     weights_on(1, far_steps[1:2])
-    product(0, frames, two)
+    product(0, 1, frames, two)
     finish_four(one[1] - 1, sz.pieces)
 
     weights_on(1, far_steps[2:])
     act4_out[...] = acts[t, 0 : sz.real]
     for p in all_pieces:
         gather_pass_on(1, acts, p, rows_of(p))
-    for p in all_pieces:
+    for p in range(*one):
         gather_here(1, acts, p, rows_of(p))
-    weights_here(1)
-    product(1, acts, one)
+    weights_here(1, 0)
+    product(1, 0, acts, one)
+    for p in range(*two):
+        gather_here(1, acts, p, rows_of(p))
     finish_five(0, one[1] - 1)
-    product(1, acts, two)
+    product(1, 0, acts, two)
     finish_five(one[1] - 1, sz.pieces)
-    spread_delta()
-
+    spread_delta(sz.pieces - 1)
     if sz.line and sz.tensor == sz.major:
-        grads_place(1, acts, 3)
-        back_products(1, lambda: grads_place(1, acts, 2))
+        back_products(1, lambda: grads_place(1, acts, 3), lambda: grads_place(1, acts, 2))
     else:
         grads_half(1, acts, True)
         back_products(1)
@@ -603,8 +614,9 @@
     @pl.loop(0, sz.pieces)
     def _(p):
         note_delta(0, p, (back_total(1, p) * slope4[rows_of(p)]).astype(BF16).astype(F32))
-
-    spread_delta()
+        pl.when(p > 0)(lambda: spread_delta(p - 1))
+
+    spread_delta(sz.pieces - 1)
     if sz.line and sz.tensor == sz.major:
         grads_place(0, frames, 3)
         grads_place(0, frames, 2)
@@ -615,7 +627,7 @@
     grads_half(0, frames, False)
     for k in near_half:
         grads_far(1, k)
-    back_products(0, lambda: grads_far(0, far_half[0]))
+    back_products(0, second=lambda: grads_far(0, far_half[0]))
     for k in (*far_half[1:], *near_half):
         grads_far(0, k)
     squares = grads_sum(1)
@@ -627,26 +639,20 @@
 
     igrad_out[...] = igrad[0 : sz.real]
 
-    squares += grads_sum(0)
-
     me = d * sz.tensor + t
-    stats_all[me, 0:1, :] = jnp.sum(squares, axis=0, keepdims=True)
     for l in (0, 1):
         stats_all[me, l + 1 : l + 2, :] = jnp.sum(bias_sum[l], axis=0, keepdims=True)
-
-    def stats_copy(k, slot):
-        other = lax.rem(me + k, sz.devices)
-        device = (lax.div(other, sz.tensor), lax.rem(other, sz.tensor))
+    squares += grads_sum(0)
+    stats_all[me, 0:1, :] = jnp.sum(squares, axis=0, keepdims=True)
+    def stats_copy(a, b, mine):
+        device = (flip_bits(d, a), flip_bits(t, b))
+        slot = me if mine else device[0] * sz.tensor + device[1]
+        k = a * sz.tensor + b
         return same(stats_all.at[slot, 0:3], st_send.at[k], st_recv.at[k], device)
 
-    def each_device(act):
-        if sz.devices <= 32:
-            for k in range(1, sz.devices):
-                act(k)
-        else:
-            pl.loop(1, sz.devices)(act)
-
-    each_device(lambda k: stats_copy(k, me).start())
+    others = [(a, b) for a in reversed(range(sz.dp)) for b in reversed(range(sz.tensor)) if a or b]
+    for a, b in others:
+        stats_copy(a, b, True).start()
 
     grads_out_rows(0)
     for l in (0, 1):
@@ -669,7 +675,8 @@
     def _(p):
         gather_sent(1, acts, p, rows_of(p))
 
-    each_device(lambda k: stats_copy(k, lax.rem(me + sz.devices - k, sz.devices)).wait_recv())
+    for a, b in others:
+        stats_copy(a, b, False).wait_recv()
 
     for q in range(sz.tensor):
         total = stats_all[q, 0:3]
@@ -677,7 +684,8 @@
             total += stats_all[slot, 0:3]
         stats_out[q, 0:3] = total
 
-    each_device(lambda k: stats_copy(k, me).wait_send())
+    for a, b in others:
+        stats_copy(a, b, True).wait_send()
 
 
 def train_step(sz, frames, item_mask, weights, biases, cotangent):
@@ -721,8 +729,8 @@
         sem((2, sz.major)),
         sem((2, sz.major)),
         sem((2,)),
-        sem((2, sz.major)),
-        sem((2, sz.major)),
+        sem((2, sz.major, 2)),
+        sem((2, sz.major, 2)),
         sem((2, sz.pieces, sz.pairs)),
         sem((2, sz.pieces, sz.pairs)),
         sem((2, sz.pieces)),

time: 82.6 us -> 81.3 us (0.984)
  Pallas kernels: 81.6 us -> 80.3 us
    pallas_call x1, Pallas kernels: 78.8 us -> 77.5 us  [train_step(): pl.pallas_call(functools.partial(body, sz), out_shape=[vmem(rows, BF16),...]
where the time goes in v6:
time: 81.3 us; the launch traced here: 81.1 us
  Pallas kernels  80.3 us (99%)
  between operations  0.86 us (1%)
    pallas_call x1, Pallas kernels, train_step(): pl.pallas_call(functools.partial(body, sz), out_shape=[vmem(rows, BF16),...  77.5 us
    pallas_call x1, Pallas kernels, finish(): pl.pallas_call(functools.partial(finish_body, sz), out_shape=[like(act4),...  2.79 us

profile of v6, /device:TPU:0, one launch (start us, length us, event | category | flops | bytes accessed | tf_op | source)
XLA Modules:
  0.0 81.1 jit_solution(9017460923099667945)
XLA Ops:
  0.6 0.0 copy-start
  0.7 0.0 copy-start.1
  0.7 0.0 copy-start.2
  0.7 77.5 %train_step.1 = (bf16[1352,128]{1,0:T(8,128)(2,1)S(1)}, bf16[1352,128]{1,0:T(8,128)(2,1)S(1)}, f32[1352,128]{1,0:T(8,128)S(1)}, f32[2,576,128]{2,1,0:T(8,128)S(1)}, f32[4,8,128]{2,1,0:T(8,128)S(1)}) custom-call(bf16[1352,128]{1,0:T(8,128)(2,1)} %bitcast.17, s32[8]{0:T(128)} %mask_ref.1, f32[2,576,128]{2,1,0:T(8,128)} %weights.1, f32[2,512]{1,0:T(2,128)} %biases_ref.3, ...), custom_call_target="tpu_custom_call" | custom-call | flops 9569304576 | bytes 6000000 | tf_op jit(solution)/shard_map/train_step/pallas_call | solution.py:754
  78.2 0.0 copy-done
  78.2 0.0 copy-done.1
  78.2 0.0 copy-done.2
  78.2 2.8 %clip_and_adamw.1 = (bf16[1352,128]{1,0:T(8,128)(2,1)}, bf16[1352,128]{1,0:T(8,128)(2,1)}, f32[1352,128]{1,0:T(8,128)}, f32[1,1]{1,0:T(1,128)}, f32[2,576,128]{2...) custom-call(bf16[1352,128]{1,0:T(8,128)(2,1)S(1)} %get-tuple-element, ...), custom_call_target="tpu_custom_call" | custom-call | flops 5000000 | bytes 7000000 | tf_op jit(solution)/shard_map/clip_and_adamw/pallas_call | solution.py:850
Async XLA Ops:
  0.6 77.5 %copy-start = (f32[2,576,128]{2,1,0:T(8,128)S(1)}, f32[2,576,128]{2,1,0:T(8,128)}, u32[]{:S(2)}) copy-start(f32[2,576,128]{2,1,0:T(8,128)} %weights.1) | copy-start | bytes 1769476
  0.7 77.5 %copy-start.1 = (f32[2,576,128]{2,1,0:T(8,128)S(1)}, f32[2,576,128]{2,1,0:T(8,128)}, u32[]{:S(2)}) copy-start(f32[2,576,128]{2,1,0:T(8,128)} %first.1) | copy-start | bytes 1769476
  0.7 77.5 %copy-start.2 = (f32[2,576,128]{2,1,0:T(8,128)S(1)}, f32[2,576,128]{2,1,0:T(8,128)}, u32[]{:S(2)}) copy-start(f32[2,576,128]{2,1,0:T(8,128)} %second.1) | copy-start | bytes 1769476

commit v7 on v6

--- a/solution.py
+++ b/solution.py
@@ -74,7 +74,7 @@
         self.line = self.major == 4
         self.far_order = (2, 1, 3) if self.line else tuple(range(1, self.major))
         cut = (TAPS + 1) // 2 * self.out
-        self.parts = (((0, cut), (cut, self.cols)), ((0, self.cols),))
+        self.parts = (((0, cut), (cut, self.cols)),) * 2
         self.devices = self.dp * self.tensor
         self.shares = 2 if self.own_in % 32 == 0 else 1
         self.share = self.own_in // self.shares
@@ -212,54 +212,61 @@
     for copy in (load_w[0], load_frames, load_w[1], load_cot, load_biases, load_mask):
         copy.start()
 
-    def weight_out(l, k):
-        return same(w_all.at[l, d], wz_send.at[l, k], wz_recv.at[l, k], far(k))
-
-    def weight_relay(l):
-        return same(w_all.at[l, far_slot(2)], wf_send.at[l], wz_recv.at[l, 3], far(1))
+    def parts_of(l):
+        return range(len(sz.parts[l]))
+
+    def weight_block(l, slot, part):
+        first, last = sz.parts[l][part]
+        return w_all.at[l, slot, :, first:last]
+
+    def weight_out(l, k, part):
+        return same(weight_block(l, d, part), wz_send.at[l, k, part], wz_recv.at[l, k, part], far(k))
+
+    def weight_relay(l, part):
+        return same(weight_block(l, far_slot(2), part), wf_send.at[l, part], wz_recv.at[l, 3, part], far(1))
 
     def weight_over(l, k, part):
-        first, last = sz.parts[l][part]
-        block = w_all.at[l, far_slot(k), :, first:last]
-        return same(block, wy_send.at[l, k, part], wy_recv.at[l, k, part], near)
+        return same(weight_block(l, far_slot(k), part), wy_send.at[l, k, part], wy_recv.at[l, k, part], near)
 
     def weights_over(l, k):
-        for part in range(len(sz.parts[l])):
+        for part in parts_of(l):
             weight_over(l, k, part).start()
 
     def weights_out(l):
         for k in sz.far_order:
-            if sz.line and k == 3:
-                pl.when(middle)(weight_out(l, k).start)
-            else:
-                weight_out(l, k).start()
+            for part in parts_of(l):
+                if sz.line and k == 3:
+                    pl.when(middle)(weight_out(l, k, part).start)
+                else:
+                    weight_out(l, k, part).start()
 
     def weights_on(l, steps):
         for k in steps:
-            same(w_all.at[l, far_slot(k)], wz_send.at[l, k], wz_recv.at[l, k], far(k)).wait_recv()
-            if sz.line and k == 2:
-                pl.when(middle)(weight_relay(l).start)
-            weights_over(l, k)
+            for part in parts_of(l):
+                block = weight_block(l, far_slot(k), part)
+                same(block, wz_send.at[l, k, part], wz_recv.at[l, k, part], far(k)).wait_recv()
+                if sz.line and k == 2:
+                    pl.when(middle)(weight_relay(l, part).start)
+                weight_over(l, k, part).start()
 
     def weights_here(l, part):
-        first, last = sz.parts[l][part]
         for k in range(sz.major):
-            block = w_all.at[l, near_slot(k), :, first:last]
+            block = weight_block(l, near_slot(k), part)
             same(block, wy_send.at[l, k, part], wy_recv.at[l, k, part], near).wait_recv()
 
     def weights_sent(l):
         for k in range(sz.major):
-            for part in range(len(sz.parts[l])):
+            for part in parts_of(l):
                 weight_over(l, k, part).wait_send()
-            if sz.line and k == 3:
-
-                @pl.when(middle)
-                def _():
-                    weight_out(l, k).wait_send()
-                    weight_relay(l).wait_send()
-
-            elif k:
-                weight_out(l, k).wait_send()
+                if sz.line and k == 3:
+
+                    @pl.when(middle)
+                    def _():
+                        weight_out(l, k, part).wait_send()
+                        weight_relay(l, part).wait_send()
+
+                elif k:
+                    weight_out(l, k, part).wait_send()
 
     def round_weights(l):
         load_w[l].wait()
@@ -406,13 +413,14 @@
                 cross_send[l, k, rows_of(p)] = total.astype(BF16)
                 cross_copy(l, p, k).start()
 
-    def back_products(l, first=None, second=None):
-        for group, meanwhile in zip(sz.groups, (first, second)):
+    def back_products(l, first=None, between=None, second=None):
+        nothing_else = lambda: None
+        for group, meanwhile, then in zip(sz.groups, (first, second), (between, None)):
             back_to_sibling(l, group)
-            if meanwhile:
-                meanwhile()
+            (meanwhile or nothing_else)()
             back_own(l, group)
             back_across(l, group)
+            (then or nothing_else)()
 
     def back_total(l, p):
         total = part_own[pair, rows_of(p)] + part_recv[l, pair, rows_of(p)].astype(F32)
@@ -448,15 +456,21 @@
     far_half = [k for k in reversed(far_steps) if k >= sz.major // 2]
     near_half = [k for k in far_steps if k < sz.major // 2]
 
-    def grads_block(l, maps, block, width, steps):
-        left = jnp.concatenate([maps[block + q] for q in range(width)], axis=1)
+    def grads_product(l, maps, block, width, first, last):
+        rows = slice(first * sz.piece, last * sz.piece)
+        left = jnp.concatenate([maps[block + q, rows] for q in range(width)], axis=1)
         into = pl.ds(block * sz.slots, width * sz.slots)
         for start in range(0, sz.cols, WIDE):
             stop = min(start + WIDE, sz.cols)
             product = lax.dot_general(
-                left, deltas[:, start:stop], (((0,), (0,)), ((), ())), preferred_element_type=F32
-            )
-            kgrad[l, into, :, start:stop] = product.reshape(width * sz.slots, sz.own_in, stop - start)
+                left, deltas[rows, start:stop], (((0,), (0,)), ((), ())), preferred_element_type=F32
+            ).reshape(width * sz.slots, sz.own_in, stop - start)
+            if first:
+                product += kgrad[l, into, :, start:stop]
+            kgrad[l, into, :, start:stop] = product
+
+    def grads_block(l, maps, block, width, steps, first=0):
+        grads_product(l, maps, block, width, first, sz.pieces)
         for k in steps:
             near_send[l, k] = kgrad[l, near_slot(k)].astype(sz.wire)
             for h in shares:
@@ -468,8 +482,8 @@
         first = (1 - own_half if other else own_half) * half
         grads_block(l, maps, first, half, far_half if other else [*near_half, 0])
 
-    def grads_place(l, maps, k):
-        grads_block(l, maps, flip_bits(major, k), 1, [k])
+    def grads_place(l, maps, k, first=0):
+        grads_block(l, maps, flip_bits(major, k), 1, [k], first)
 
     def relay_copy(l, h):
         rows = share_of(h)
@@ -477,8 +491,8 @@
             far_send.at[l, 3, rows], relay_recv.at[l, rows], gz_send.at[l, 3, h], gr_recv.at[l, h], far(1)
         )
 
-    def grads_far(l, k):
-        for h in shares:
+    def grads_far(l, k, some=shares):
+        for h in some:
             rows = share_of(h)
             near_copy(l, k, h).wait_recv()
             total = kgrad[l, far_slot(k), rows] + near_recv[l, k, rows].astype(F32)
@@ -580,8 +594,8 @@
     weights_here(0, 0)
     product(0, 0, frames, one)
     product(0, 0, frames, two)
+    weights_on(1, far_steps[:1])
     weights_here(0, 1)
-    weights_on(1, far_steps[:1])
     product(0, 1, frames, one)
     finish_four(0, one[1] - 1)
     weights_on(1, far_steps[1:2])
@@ -596,40 +610,57 @@
         gather_here(1, acts, p, rows_of(p))
     weights_here(1, 0)
     product(1, 0, acts, one)
+    weights_here(1, 1)
+    product(1, 1, acts, one)
     for p in range(*two):
         gather_here(1, acts, p, rows_of(p))
     finish_five(0, one[1] - 1)
     product(1, 0, acts, two)
+    product(1, 1, acts, two)
     finish_five(one[1] - 1, sz.pieces)
     spread_delta(sz.pieces - 1)
     if sz.line and sz.tensor == sz.major:
-        back_products(1, lambda: grads_place(1, acts, 3), lambda: grads_place(1, acts, 2))
+        back_products(1, lambda: grads_place(1, acts, 3), second=lambda: grads_place(1, acts, 2))
     else:
         grads_half(1, acts, True)
         back_products(1)
+    grads_far(1, far_half[0], shares[:1])
     grads_half(1, acts, False)
-    act5_out[...] = act5[0 : sz.real]
-    grads_far(1, far_half[0])
-
-    @pl.loop(0, sz.pieces)
-    def _(p):
-        note_delta(0, p, (back_total(1, p) * slope4[rows_of(p)]).astype(BF16).astype(F32))
-        pl.when(p > 0)(lambda: spread_delta(p - 1))
-
-    spread_delta(sz.pieces - 1)
-    if sz.line and sz.tensor == sz.major:
-        grads_place(0, frames, 3)
-        grads_place(0, frames, 2)
+    grads_far(1, far_half[0], shares[1:])
+
+    def delta_four(first, last):
+        @pl.loop(first, last)
+        def _(p):
+            note_delta(0, p, (back_total(1, p) * slope4[rows_of(p)]).astype(BF16).astype(F32))
+            pl.when(p > 0)(lambda: spread_delta(p - 1))
+
+    if sz.line and sz.tensor == sz.major and sz.pieces > 2:
+        early = sz.pieces - 2
+        delta_four(0, sz.pieces - 1)
+        grads_far(1, 2)
+        for k in (3, 2):
+            grads_product(0, frames, flip_bits(major, k), 1, 0, early)
+        delta_four(sz.pieces - 1, sz.pieces)
+        spread_delta(sz.pieces - 1)
+        grads_place(0, frames, 3, early)
+        grads_place(0, frames, 2, early if 2 in (3, 2) else 0)
     else:
+        delta_four(0, sz.pieces)
+        spread_delta(sz.pieces - 1)
         grads_half(0, frames, True)
-    for k in far_half[1:]:
+        for k in far_half[1:]:
+            grads_far(1, k)
+    for k in near_half:
         grads_far(1, k)
     grads_half(0, frames, False)
-    for k in near_half:
-        grads_far(1, k)
-    back_products(0, second=lambda: grads_far(0, far_half[0]))
+    back_products(
+        0,
+        between=lambda: grads_far(0, far_half[0], shares[:1]),
+        second=lambda: grads_far(0, far_half[0], shares[1:]),
+    )
     for k in (*far_half[1:], *near_half):
         grads_far(0, k)
+    act5_out[...] = act5[0 : sz.real]
     squares = grads_sum(1)
     grads_out_rows(1)
 
@@ -726,9 +757,9 @@
         vmem((sz.devices, 8, sz.out), F32),
         sem((6,)),
         pltpu.SemaphoreType.REGULAR,
-        sem((2, sz.major)),
-        sem((2, sz.major)),
-        sem((2,)),
+        sem((2, sz.major, 2)),
+        sem((2, sz.major, 2)),
+        sem((2, 2)),
         sem((2, sz.major, 2)),
         sem((2, sz.major, 2)),
         sem((2, sz.pieces, sz.pairs)),

time: 81.3 us -> 79.4 us (0.977)
  Pallas kernels: 80.3 us -> 78.3 us
    pallas_call x1, Pallas kernels: 77.5 us -> 75.6 us  [train_step(): pl.pallas_call(functools.partial(body, sz), out_shape=[vmem(rows, BF16),...]
where the time goes in v7:
time: 79.4 us; the launch traced here: 79.2 us
  Pallas kernels  78.3 us (99%)
  between operations  0.86 us (1%)
    pallas_call x1, Pallas kernels, train_step(): pl.pallas_call(functools.partial(body, sz), out_shape=[vmem(rows, BF16),...  75.6 us
    pallas_call x1, Pallas kernels, finish(): pl.pallas_call(functools.partial(finish_body, sz), out_shape=[like(act4),...  2.79 us

profile of v7, /device:TPU:0, one launch (start us, length us, event | category | flops | bytes accessed | tf_op | source)
XLA Modules:
  0.0 79.2 jit_solution(17988761037427822122)
XLA Ops:
  0.6 0.0 copy-start
  0.7 0.0 copy-start.1
  0.7 0.0 copy-start.2
  0.7 75.6 %train_step.1 = (bf16[1352,128]{1,0:T(8,128)(2,1)S(1)}, bf16[1352,128]{1,0:T(8,128)(2,1)S(1)}, f32[1352,128]{1,0:T(8,128)S(1)}, f32[2,576,128]{2,1,0:T(8,128)S(1)}, f32[4,8,128]{2,1,0:T(8,128)S(1)}) custom-call(bf16[1352,128]{1,0:T(8,128)(2,1)} %bitcast.17, s32[8]{0:T(128)} %mask_ref.1, f32[2,576,128]{2,1,0:T(8,128)} %weights.1, f32[2,512]{1,0:T(2,128)} %biases_ref.3, ...), custom_call_target="tpu_custom_call" | custom-call | flops 9569304576 | bytes 6000000 | tf_op jit(solution)/shard_map/train_step/pallas_call | solution.py:785
  76.2 0.0 copy-done
  76.3 0.0 copy-done.1
  76.3 0.0 copy-done.2
  76.3 2.8 %clip_and_adamw.1 = (bf16[1352,128]{1,0:T(8,128)(2,1)}, bf16[1352,128]{1,0:T(8,128)(2,1)}, f32[1352,128]{1,0:T(8,128)}, f32[1,1]{1,0:T(1,128)}, f32[2,576,128]{2...) custom-call(bf16[1352,128]{1,0:T(8,128)(2,1)S(1)} %get-tuple-element, ...), custom_call_target="tpu_custom_call" | custom-call | flops 5000000 | bytes 7000000 | tf_op jit(solution)/shard_map/clip_and_adamw/pallas_call | solution.py:881
Async XLA Ops:
  0.6 75.6 %copy-start = (f32[2,576,128]{2,1,0:T(8,128)S(1)}, f32[2,576,128]{2,1,0:T(8,128)}, u32[]{:S(2)}) copy-start(f32[2,576,128]{2,1,0:T(8,128)} %weights.1) | copy-start | bytes 1769476
  0.7 75.6 %copy-start.1 = (f32[2,576,128]{2,1,0:T(8,128)S(1)}, f32[2,576,128]{2,1,0:T(8,128)}, u32[]{:S(2)}) copy-start(f32[2,576,128]{2,1,0:T(8,128)} %first.1) | copy-start | bytes 1769476
  0.7 75.6 %copy-start.2 = (f32[2,576,128]{2,1,0:T(8,128)S(1)}, f32[2,576,128]{2,1,0:T(8,128)}, u32[]{:S(2)}) copy-start(f32[2,576,128]{2,1,0:T(8,128)} %second.1) | copy-start | bytes 1769476

commit v8 on v7

--- a/solution.py
+++ b/solution.py
@@ -602,9 +602,10 @@
     product(0, 1, frames, two)
     finish_four(one[1] - 1, sz.pieces)
 
+    for p in all_pieces[:1]:
+        gather_pass_on(1, acts, p, rows_of(p))
     weights_on(1, far_steps[2:])
-    act4_out[...] = acts[t, 0 : sz.real]
-    for p in all_pieces:
+    for p in all_pieces[1:]:
         gather_pass_on(1, acts, p, rows_of(p))
     for p in range(*one):
         gather_here(1, acts, p, rows_of(p))
@@ -612,9 +613,9 @@
     product(1, 0, acts, one)
     weights_here(1, 1)
     product(1, 1, acts, one)
+    finish_five(0, one[1] - 1)
     for p in range(*two):
         gather_here(1, acts, p, rows_of(p))
-    finish_five(0, one[1] - 1)
     product(1, 0, acts, two)
     product(1, 1, acts, two)
     finish_five(one[1] - 1, sz.pieces)
@@ -643,7 +644,7 @@
         delta_four(sz.pieces - 1, sz.pieces)
         spread_delta(sz.pieces - 1)
         grads_place(0, frames, 3, early)
-        grads_place(0, frames, 2, early if 2 in (3, 2) else 0)
+        grads_place(0, frames, 2, early)
     else:
         delta_four(0, sz.pieces)
         spread_delta(sz.pieces - 1)
@@ -660,6 +661,7 @@
     )
     for k in (*far_half[1:], *near_half):
         grads_far(0, k)
+    act4_out[...] = acts[t, 0 : sz.real]
     act5_out[...] = act5[0 : sz.real]
     squares = grads_sum(1)
     grads_out_rows(1)

time: 79.4 us -> 79.3 us (level)
  no operation moved by 1% of the time
where the time goes in v8:
time: 79.3 us; the launch traced here: 79.1 us
  Pallas kernels  78.3 us (99%)
  between operations  0.86 us (1%)
    pallas_call x1, Pallas kernels, train_step(): pl.pallas_call(functools.partial(body, sz), out_shape=[vmem(rows, BF16),...  75.5 us
    pallas_call x1, Pallas kernels, finish(): pl.pallas_call(functools.partial(finish_body, sz), out_shape=[like(act4),...  2.79 us

profile of v8, /device:TPU:0, one launch (start us, length us, event | category | flops | bytes accessed | tf_op | source)
XLA Modules:
  0.0 79.1 jit_solution(15081581207571326070)
XLA Ops:
  0.6 0.0 copy-start
  0.7 0.0 copy-start.1
  0.7 0.0 copy-start.2
  0.7 75.5 %train_step.1 = (bf16[1352,128]{1,0:T(8,128)(2,1)S(1)}, bf16[1352,128]{1,0:T(8,128)(2,1)S(1)}, f32[1352,128]{1,0:T(8,128)S(1)}, f32[2,576,128]{2,1,0:T(8,128)S(1)}, f32[4,8,128]{2,1,0:T(8,128)S(1)}) custom-call(bf16[1352,128]{1,0:T(8,128)(2,1)} %bitcast.17, s32[8]{0:T(128)} %mask_ref.1, f32[2,576,128]{2,1,0:T(8,128)} %weights.1, f32[2,512]{1,0:T(2,128)} %biases_ref.3, ...), custom_call_target="tpu_custom_call" | custom-call | flops 9569304576 | bytes 6000000 | tf_op jit(solution)/shard_map/train_step/pallas_call | solution.py:787
  76.2 0.0 copy-done
  76.2 0.0 copy-done.1
  76.2 0.0 copy-done.2
  76.2 2.8 %clip_and_adamw.1 = (bf16[1352,128]{1,0:T(8,128)(2,1)}, bf16[1352,128]{1,0:T(8,128)(2,1)}, f32[1352,128]{1,0:T(8,128)}, f32[1,1]{1,0:T(1,128)}, f32[2,576,128]{2...) custom-call(bf16[1352,128]{1,0:T(8,128)(2,1)S(1)} %get-tuple-element, ...), custom_call_target="tpu_custom_call" | custom-call | flops 5000000 | bytes 7000000 | tf_op jit(solution)/shard_map/clip_and_adamw/pallas_call | solution.py:883
Async XLA Ops:
  0.6 75.5 %copy-start = (f32[2,576,128]{2,1,0:T(8,128)S(1)}, f32[2,576,128]{2,1,0:T(8,128)}, u32[]{:S(2)}) copy-start(f32[2,576,128]{2,1,0:T(8,128)} %weights.1) | copy-start | bytes 1769476
  0.7 75.5 %copy-start.1 = (f32[2,576,128]{2,1,0:T(8,128)S(1)}, f32[2,576,128]{2,1,0:T(8,128)}, u32[]{:S(2)}) copy-start(f32[2,576,128]{2,1,0:T(8,128)} %first.1) | copy-start | bytes 1769476
  0.7 75.5 %copy-start.2 = (f32[2,576,128]{2,1,0:T(8,128)S(1)}, f32[2,576,128]{2,1,0:T(8,128)}, u32[]{:S(2)}) copy-start(f32[2,576,128]{2,1,0:T(8,128)} %second.1) | copy-start | bytes 1769476

commit v9 on v8

--- a/solution.py
+++ b/solution.py
@@ -23,7 +23,7 @@
 ROOT = math.sqrt(2.0 / math.pi)
 CUBE = 0.044715
 TAPS = 9
-WIDE = 256
+WIDE = 512
 
 
 def gelu_parts(value):

time: 79.3 us -> 79.3 us (level)
  no operation moved by 1% of the time
where the time goes in v9:
time: 79.3 us; the launch traced here: 79.1 us
  Pallas kernels  78.3 us (99%)
  between operations  0.86 us (1%)
    pallas_call x1, Pallas kernels, train_step(): pl.pallas_call(functools.partial(body, sz), out_shape=[vmem(rows, BF16),...  75.5 us
    pallas_call x1, Pallas kernels, finish(): pl.pallas_call(functools.partial(finish_body, sz), out_shape=[like(act4),...  2.79 us

profile of v9, /device:TPU:0, one launch (start us, length us, event | category | flops | bytes accessed | tf_op | source)
XLA Modules:
  0.0 79.1 jit_solution(15081581207571326070)
XLA Ops:
  0.6 0.0 copy-start
  0.7 0.0 copy-start.1
  0.7 0.0 copy-start.2
  0.7 75.5 %train_step.1 = (bf16[1352,128]{1,0:T(8,128)(2,1)S(1)}, bf16[1352,128]{1,0:T(8,128)(2,1)S(1)}, f32[1352,128]{1,0:T(8,128)S(1)}, f32[2,576,128]{2,1,0:T(8,128)S(1)}, f32[4,8,128]{2,1,0:T(8,128)S(1)}) custom-call(bf16[1352,128]{1,0:T(8,128)(2,1)} %bitcast.17, s32[8]{0:T(128)} %mask_ref.1, f32[2,576,128]{2,1,0:T(8,128)} %weights.1, f32[2,512]{1,0:T(2,128)} %biases_ref.3, ...), custom_call_target="tpu_custom_call" | custom-call | flops 9569304576 | bytes 6000000 | tf_op jit(solution)/shard_map/train_step/pallas_call | solution.py:787
  76.2 0.0 copy-done
  76.2 0.0 copy-done.1
  76.2 0.0 copy-done.2
  76.2 2.8 %clip_and_adamw.1 = (bf16[1352,128]{1,0:T(8,128)(2,1)}, bf16[1352,128]{1,0:T(8,128)(2,1)}, f32[1352,128]{1,0:T(8,128)}, f32[1,1]{1,0:T(1,128)}, f32[2,576,128]{2...) custom-call(bf16[1352,128]{1,0:T(8,128)(2,1)S(1)} %get-tuple-element, ...), custom_call_target="tpu_custom_call" | custom-call | flops 5000000 | bytes 7000000 | tf_op jit(solution)/shard_map/clip_and_adamw/pallas_call | solution.py:883
Async XLA Ops:
  0.6 75.5 %copy-start = (f32[2,576,128]{2,1,0:T(8,128)S(1)}, f32[2,576,128]{2,1,0:T(8,128)}, u32[]{:S(2)}) copy-start(f32[2,576,128]{2,1,0:T(8,128)} %weights.1) | copy-start | bytes 1769476
  0.7 75.5 %copy-start.1 = (f32[2,576,128]{2,1,0:T(8,128)S(1)}, f32[2,576,128]{2,1,0:T(8,128)}, u32[]{:S(2)}) copy-start(f32[2,576,128]{2,1,0:T(8,128)} %first.1) | copy-start | bytes 1769476
  0.7 75.5 %copy-start.2 = (f32[2,576,128]{2,1,0:T(8,128)S(1)}, f32[2,576,128]{2,1,0:T(8,128)}, u32[]{:S(2)}) copy-start(f32[2,576,128]{2,1,0:T(8,128)} %second.1) | copy-start | bytes 1769476
